TPU v7x, 32 devices: a whole 2x2x4 slice. The times are simulated.
32 devices in a mesh: row: 4 (over z), col: 8 (over y, x, core).
Axes of the slice: x: 2, y: 2, z: 4, core: 2. Of those that a mesh axis runs over, the one named last changes fastest.
Arguments:
- block: float32 [2048, 1024], P('row', 'col'), may hold values from -6 to 6
- panels: float32 [2, 2048, 256], P(None, 'row', 'col'), may hold values from -0.125 to 0.125
- pivots: int32 [2, 256], replicated, may hold values from 0 to 2047, as said below
Outputs:
- updated: float32 [2048, 1024], P('row', 'col')
Inputs may be any that keep to these rules, and one draw needn't show every extreme that they name: `pivots`: entry j of list k is either k*256+j itself or a global row at or beyond (k+1)*256; within one list the entries beyond are all different; entry 0 of list 0 is 0 and entry 255 of list 0 is 2047.
All inputs are finite; a program needn't handle non-finite values.
Results may differ from a plain program's by a relative error of at most 0.0001.
Values sent between devices are 32-bit elements; how exact they have to be, the bound alone decides.
A program may use at most 64 MiB of HBM per device.

v0:
```python
import jax
import jax.numpy as jnp
from jax import lax
from jax.sharding import PartitionSpec as P

PW = 256


def swap_order(piv_row, offset, count):
    own = offset + jnp.arange(piv_row.shape[0], dtype=jnp.int32)
    base = jnp.arange(count, dtype=jnp.int32)
    return base.at[own].set(piv_row).at[piv_row].set(own)


def pick_rows(data, perm, targets, start):
    local_src = perm[targets] - start
    owned = (local_src >= 0) & (local_src < data.shape[0])
    taken = jnp.take(data, jnp.clip(local_src, 0, data.shape[0] - 1), axis=0)
    return jnp.where(owned[:, None], taken, 0.0)


def place_rows(data, targets, values, start):
    local_dst = targets - start
    inside = (local_dst >= 0) & (local_dst < data.shape[0])
    where_to = jnp.where(inside, local_dst, data.shape[0])
    return data.at[where_to].set(values, mode="drop")


def solve_top(diag_rows, rows):
    strict = jnp.tril(diag_rows, -1)
    inverse = jnp.eye(PW, dtype=jnp.float32) - strict
    power = strict
    for level in range(1, PW.bit_length() - 1):
        power = jnp.dot(
            power, power, precision=lax.Precision.HIGHEST, preferred_element_type=jnp.float32
        )
        inverse = inverse + jnp.dot(
            inverse, power, precision=lax.Precision.HIGHEST, preferred_element_type=jnp.float32
        )
    return jnp.dot(
        inverse, rows, precision=lax.Precision.HIGHEST, preferred_element_type=jnp.float32
    )


def finish(work, lower, offset, start, upper):
    product = jnp.dot(
        lower, upper, precision=lax.Precision.HIGHEST, preferred_element_type=jnp.float32
    )
    global_rows = start + jnp.arange(work.shape[0], dtype=jnp.int32)
    work = jnp.where((global_rows >= offset + PW)[:, None], work - product, work)
    placed = work.at[offset : offset + PW].set(upper)
    in_top = (global_rows >= offset) & (global_rows < offset + PW)
    return jnp.where(in_top[:, None], placed, work)


def body(block, panels, pivots):
    rows_here = block.shape[0]
    rows_all = rows_here * lax.axis_size("row")
    start = lax.axis_index("row") * rows_here
    identity_perm = jnp.arange(rows_all, dtype=jnp.int32)
    perms = [swap_order(pivots[panel], panel * PW, rows_all) for panel in range(2)]
    targets = [
        jnp.concatenate([jnp.arange(panel * PW, panel * PW + PW, dtype=jnp.int32), pivots[panel]])
        for panel in range(2)
    ]
    tops_index = [jnp.arange(panel * PW, panel * PW + PW, dtype=jnp.int32) for panel in range(2)]
    work = block
    lowers = lax.all_gather(panels, "col", axis=2, tiled=True)
    for panel in range(2):
        offset = panel * PW
        diag_rows = pick_rows(lowers[panel], identity_perm, tops_index[panel], start)
        picked = pick_rows(work, perms[panel], targets[panel], start)
        moved, diag_all = lax.psum((picked, diag_rows), "row")
        work = place_rows(work, targets[panel], moved, start)
        upper = solve_top(diag_all, moved[:PW])
        work = finish(work, lowers[panel], offset, start, upper)
    return work


def solution(mesh):
    return jax.shard_map(
        body,
        mesh=mesh,
        in_specs=(P("row", "col"), P(None, "row", "col"), P()),
        out_specs=P("row", "col"),
        check_vma=False,
    )
```

profile of v0, /device:TPU:0, one launch (start us, length us, event | category | flops | bytes accessed | tf_op | source)
XLA Modules:
  0.0 148.8 jit_solution(16834362578277802717)
XLA Ops:
  6.5 1.0 copy.32
  7.5 0.7 copy.10
  8.4 0.6 copy-done.5
  9.1 1.4 scatter_fusion
  10.5 1.4 scatter_fusion.1
  11.9 3.1 %gather_fusion = s32[512]{0:T(512)S(1)} fusion(s32[2048]{0:T(1024)S(1)} %scatter_fusion.1, s32[1024]{0:T(1024)S(1)} %pad_clamp_fusion.7), kind=kCustom, calls=%fused_computation.4 | custom fusion | bytes 6144 | tf_op jit(solution)/shard_map/gather | solution.py:16
  15.1 1.0 gather_fusion.4
  16.2 1.7 %gather_fusion.3 = s32[256]{0:T(256)S(1)} fusion(s32[2048]{0:T(1024)S(1)} %iota.131, s32[1024]{0:T(1024)S(1)} %pad_clamp_fusion.1), kind=kCustom, calls=%fused_computation.7 | custom fusion | bytes 3072 | tf_op jit(solution)/shard_map/gather | solution.py:16
  18.0 1.7 %gather_fusion.1 = s32[256]{0:T(256)S(1)} fusion(s32[2048]{0:T(1024)S(1)} %iota.125, s32[1024]{0:T(1024)S(1)} %pad_clamp_fusion.5), kind=kCustom, calls=%fused_computation.5 | custom fusion | bytes 3072 | tf_op jit(solution)/shard_map/gather | solution.py:16
  19.7 1.4 scatter_fusion.3
  21.1 1.4 scatter_fusion.4
  22.6 3.1 %gather_fusion.2 = s32[512]{0:T(512)S(1)} fusion(s32[2048]{0:T(1024)S(1)} %scatter_fusion.4, s32[1024]{0:T(1024)S(1)} %pad_clamp_fusion.3), kind=kCustom, calls=%fused_computation.6 | custom fusion | bytes 6144 | tf_op jit(solution)/shard_map/gather | solution.py:16
  25.8 0.9 select_select_fusion.3
  26.7 8.7 %all-gather.2.cloned.1.call-done = f32[2,512,256]{1,0,2:T(2,128)} async-done(((f32[2,512,32]{1,0,2:T(2,128)}), f32[2,512,256]{1,0,2:T(2,128)}) %all-gather.2.cloned.1.call-update) | async-done | bytes 1048592 | tf_op jit(solution)/shard_map/all_gather | solution.py:68
  35.5 2.5 %fusion.34 = (f32[1,512,256]{1,0,2:T(1,128)S(1)}, f32[1,512,256]{1,0,2:T(1,128)S(1)}) fusion(f32[2,512,256]{1,0,2:T(2,128)} %all-gather.2.cloned.1.call-done), kind=kLoop, calls=%fused_computation.111 | loop fusion | bytes 2097152 | tf_op jit(solution)/shard_map/slice | solution.py:76
  37.9 0.5 copy.17
  38.4 1.0 gather_fusion.5
  39.4 0.8 select_select_fusion.2
  40.3 0.2 all-reduce.5.cloned.1.call-start
  40.6 0.5 copy.18
  41.1 1.0 gather_fusion.7
  42.0 0.8 select_select_fusion
  42.9 36.1 %all-reduce.7.cloned.1.call-done = (f32[512,128]{1,0:T(8,128)}, f32[256,256]{1,0:T(8,128)}) async-done(((f32[512,128]{1,0:T(8,128)}, f32[256,256]{1,0:T(8,128)}), (f32[512,128]{1,0:T(8,128)}, f32[256,256]{1,0:T(8,128)})) %all-reduce.7.cloned.1.call-update) | async-done | bytes 524304 | tf_op jit(solution)/shard_map/psum | solution.py:73
  78.9 1.6 %fusion.6 = f32[256,256]{1,0:T(8,128)S(1)} fusion(f32[256,256]{1,0:T(8,128)} %get-tuple-element.36, s32[256]{0:T(256)S(1)} %iota_add_fusion.5), kind=kOutput, calls=%fused_computation.44 | convolution fusion | flops 201457664 | bytes 525312 | tf_op jit(solution)/shard_map/dot_general | solution.py:34
  80.5 0.4 convolution_add_fusion.13
  80.9 0.4 fusion.36
  81.3 0.4 fusion.37
  81.7 0.4 convolution_add_fusion.12
  82.1 0.4 fusion.38
  82.5 0.4 convolution_add_fusion.11
  82.9 0.4 fusion.39
  83.3 0.4 convolution_add_fusion.10
  83.7 0.4 fusion.40
  84.0 0.4 convolution_add_fusion.9
  84.4 0.4 fusion.41
  84.8 0.4 convolution_add_fusion.8
  85.2 0.6 copy-done.2
  85.8 2.0 %scatter_fusion.2 = f32[512,128]{1,0:T(8,128)S(1)} fusion(f32[512,128]{1,0:T(8,128)S(1)} %copy.32, s32[512]{0:T(512)S(1)} %bitcast.91, f32[512,128]{1,0:T(8,128)S(1)} %copy-done.2), kind=kCustom, calls=%fused_computation.10 | custom fusion | bytes 788480 | tf_op jit(solution)/shard_map/scatter | solution.py:26
  87.8 0.4 convolution_add_fusion.7
  88.2 0.4 fusion.16
  88.6 0.6 fusion.3
  89.2 0.1 fusion.15
  89.3 1.0 gather_fusion.6
  90.4 0.9 select_select_fusion.1
  91.3 38.6 %all-reduce.5.cloned.1.call-done = (f32[512,128]{1,0:T(8,128)}, f32[256,256]{1,0:T(8,128)}) async-done(((f32[512,128]{1,0:T(8,128)}, f32[256,256]{1,0:T(8,128)}), (f32[512,128]{1,0:T(8,128)}, f32[256,256]{1,0:T(8,128)})) %all-reduce.5.cloned.1.call-update) | async-done | bytes 524304 | tf_op jit(solution)/shard_map/psum | solution.py:73
  129.9 1.6 %fusion.9 = f32[256,256]{1,0:T(8,128)S(1)} fusion(f32[256,256]{1,0:T(8,128)} %get-tuple-element.34, s32[256]{0:T(256)S(1)} %iota_add_fusion.5), kind=kOutput, calls=%fused_computation.45 | convolution fusion | flops 201457664 | bytes 525312 | tf_op jit(solution)/shard_map/dot_general | solution.py:34
  131.5 0.4 convolution_add_fusion.6
  131.9 0.4 fusion.42
  132.3 0.4 fusion.43
  132.7 0.4 convolution_add_fusion.5
  133.1 0.4 fusion.44
  133.4 0.4 convolution_add_fusion.4
  133.8 0.4 fusion.45
  134.2 0.4 convolution_add_fusion.3
  134.6 0.4 fusion.46
  135.0 0.4 convolution_add_fusion.2
  135.4 0.4 fusion.47
  135.8 0.4 convolution_add_fusion.1
  136.2 0.6 copy-done.3
  136.7 1.8 %scatter_fusion.5 = f32[512,128]{1,0:T(8,128)S(1)} fusion(f32[512,128]{1,0:T(8,128)S(1)} %fusion.15, s32[512]{0:T(512)S(1)} %bitcast.90, f32[512,128]{1,0:T(8,128)S(1)} %copy-done.3), kind=kCustom, calls=%fused_computation.13 | custom fusion | bytes 788480 | tf_op jit(solution)/shard_map/scatter | solution.py:26
  138.5 0.4 convolution_add_fusion
  138.9 0.4 fusion.13
  139.3 1.3 fusion.1
  140.6 1.7 %fusion.12 = f32[512,128]{1,0:T(8,128)} fusion(f32[512,128]{1,0:T(8,128)} %fusion.1, f32[256,128]{1,0:T(8,128)S(1)} %fusion.13, pred[256]{0:T(512)(128)(4,1)S(1)} %get-tuple-element.31), kind=kLoop, calls=%fused_computation.47 | loop fusion | flops 32768 | bytes 393472 | tf_op jit(solution)/shard_map/jit(_where)/select_n | solution.py:53
  (43 shorter events, 0.3 us)
Async XLA Ops:
  6.5 1.0 copy-start.4
  6.5 28.9 %all-gather.2.cloned.1.call-start = ((), (), s32[]{:S(2)}) async-start(), calls=%async_computation | async-start | bytes 1179648 | tf_op jit(solution)/shard_map/all_gather | solution.py:68
  8.3 0.7 copy-start.5
  8.3 70.6 %all-reduce.7.cloned.1.call-start = ((), (), s32[]{:S(2)}) async-start(), calls=%async_computation.2 | async-start | bytes 1048576 | tf_op jit(solution)/shard_map/psum | solution.py:73
  40.3 89.6 %all-reduce.5.cloned.1.call-start = ((), (), s32[]{:S(2)}) async-start(), calls=%async_computation.1 | async-start | bytes 1048576 | tf_op jit(solution)/shard_map/psum | solution.py:73
  78.9 1.6 %copy-start = (f32[256,256]{1,0:T(8,128)S(1)}, f32[256,256]{1,0:T(8,128)}, u32[]{:S(2)}) copy-start(f32[256,256]{1,0:T(8,128)} %get-tuple-element.36) | copy-start | bytes 786436
  84.8 1.0 copy-start.2
  129.9 1.6 %copy-start.1 = (f32[256,256]{1,0:T(8,128)S(1)}, f32[256,256]{1,0:T(8,128)}, u32[]{:S(2)}) copy-start(f32[256,256]{1,0:T(8,128)} %get-tuple-element.34) | copy-start | bytes 786436
  135.8 1.0 copy-start.3
Sparse Core Ops, SparseCore 0:
  9.2 26.1 all-gather.1
  40.4 38.4 all-reduce.6
  91.4 38.4 all-reduce.4
where the time goes:
time: 149 us
  waiting for transfers between devices  83.4 us (56%)
  local copies, waits for them, and re-layouts  30.2 us (20%)
  matrix products  15.7 us (11%)
  between operations  13.7 us (9%)
  other arithmetic  5.41 us (4%)
    psum x2, waiting for transfers between devices, body(): moved, diag_all = lax.psum((picked, diag_rows), 'row')  74.6 us
    gather x4, local copies, waits for them, and re-layouts, pick_rows(): local_src = perm[targets] - start  9.73 us
    all_gather x1, waiting for transfers between devices, body(): lowers = lax.all_gather(panels, 'col', axis=2, tiled=True)  8.74 us
    dot_general x14, matrix products, solve_top(): jnp.dot(power, power, precision=lax.Precision.HIGHEST, preferred_element_...  7.7 us
    scatter x4, local copies, waits for them, and re-layouts, swap_order(): return base.at[own].set(piv_row).at[piv_row].set(own)  5.68 us
    dot_general x14, matrix products, solve_top(): jnp.dot(inverse, power, precision=lax.Precision.HIGHEST, preferred_elemen...  5.41 us
    unnamed x16, local copies, waits for them, and re-layouts  4.46 us
    gather x4, local copies, waits for them, and re-layouts, pick_rows(): taken = jnp.take(data, jnp.clip(local_src, 0, data.shape[0] - 1), axis=0)  4.01 us
  transfers between devices with their start and end apart: 3, of which 3 were waited for; matrix products, arithmetic and copies ran while one was open for 13% of the time, Pallas kernels for 0%

commit v1 on v0

--- a/solution.py
+++ b/solution.py
@@ -1,6 +1,10 @@
+import functools
+
 import jax
 import jax.numpy as jnp
 from jax import lax
+from jax.experimental import pallas as pl
+from jax.experimental.pallas import tpu as pltpu
 from jax.sharding import PartitionSpec as P
 
 PW = 256
@@ -53,7 +57,7 @@
     return jnp.where(in_top[:, None], placed, work)
 
 
-def body(block, panels, pivots):
+def plain(block, panels, pivots):
     rows_here = block.shape[0]
     rows_all = rows_here * lax.axis_size("row")
     start = lax.axis_index("row") * rows_here
@@ -76,6 +80,414 @@
         work = finish(work, lowers[panel], offset, start, upper)
     return work
 
+MESH = pl.DeviceIdType.MESH
+F32, BF16 = jnp.float32, jnp.bfloat16
+CHUNKS = 4
+
+
+def dot(a, b):
+    return jnp.dot(a, b, preferred_element_type=F32)
+
+
+def split(a):
+    high = a.astype(BF16)
+    return high, (a - high.astype(F32)).astype(BF16)
+
+
+def dot_split(a, b):
+    a_high, a_low = a
+    b_high, b_low = b
+    return dot(a_high, b_high) + (dot(a_high, b_low) + dot(a_low, b_high))
+
+
+def dot_pick(a, one_hot):
+    m = a.shape[0]
+    high, rest = a.astype(BF16), None
+    rest = a - high.astype(F32)
+    mid = rest.astype(BF16)
+    low = (rest - mid.astype(F32)).astype(BF16)
+    out = dot(jnp.concatenate([high, mid, low], 0), one_hot)
+    return out[:m] + (out[m : 2 * m] + out[2 * m :])
+
+
+def iota(shape, dim):
+    return lax.broadcasted_iota(jnp.int32, shape, dim)
+
+
+def one_hot(condition):
+    return jnp.where(condition, 1.0, 0.0)
+
+
+def invert_upper(upper_part):
+    n = upper_part.shape[0]
+    row, col = iota((n, n), 0), iota((n, n), 1)
+    strict = jnp.where(row < col, upper_part, 0.0)
+    size = 32
+    power = jnp.where(row // size == col // size, strict, 0.0)
+    inverse = one_hot(row == col) - power
+    span = 2
+    while span < size:
+        parts = split(power)
+        power = dot_split(parts, parts)
+        inverse = inverse + dot_split(split(inverse), split(power))
+        span *= 2
+    while size < n:
+        pair = (row // (2 * size) == col // (2 * size)) & (row // size != col // size)
+        parts = split(inverse)
+        right = dot_split(split(jnp.where(pair, strict, 0.0)), parts)
+        inverse = inverse - dot_split(parts, split(right))
+        size *= 2
+    return inverse
+
+
+def kernel(
+    n_row, n_col, piv_ref, block_ref, panels_ref, out_ref,
+    g_diag, g_top, g_one, g_zero, v_in, v_out, s_in, s_out, vl_in, vl_out, sl_in, sl_out,
+    d_sem, vl_sem, sl_sem, v_sem, s_sem, peer_send, peer_recv, sib_send, sib_recv,
+):
+    r, c = lax.axis_index("row"), lax.axis_index("col")
+    rows, cols = block_ref.shape
+    tops = 2 * PW
+    kc = panels_ref.shape[2]
+    n_peer = n_col // 2
+    sibling = c + 1 - 2 * (c % 2)
+    is_first, is_last = r == 0, r == n_row - 1
+    start = r * rows
+
+    barrier = pltpu.get_barrier_semaphore()
+
+    @pl.when(r > 0)
+    def _():
+        pl.semaphore_signal(barrier, 1, device_id={"row": r - 1}, device_id_type=MESH)
+
+    @pl.when(r < n_row - 1)
+    def _():
+        pl.semaphore_signal(barrier, 1, device_id={"row": r + 1}, device_id_type=MESH)
+
+    for m in range(1, n_peer):
+        pl.semaphore_signal(barrier, 1, device_id={"col": (c + 2 * m) % n_col}, device_id_type=MESH)
+    pl.semaphore_signal(barrier, 1, device_id={"col": sibling}, device_id_type=MESH)
+
+    zero_t, one_t = panels_ref[0].T, panels_ref[1].T
+    block_t = block_ref[...].T
+    g_one[c] = one_t
+
+    @pl.when(is_first)
+    def _():
+        g_diag[c, 0] = zero_t[:, :PW]
+        g_diag[c, 1] = one_t[:, PW:tops]
+
+    @pl.when((r > 0) & (r < n_row - 1))
+    def _():
+        pl.semaphore_wait(barrier, n_peer + 2)
+
+    @pl.when(is_first | is_last)
+    def _():
+        pl.semaphore_wait(barrier, n_peer + 1)
+
+    def hop(src, dst, sem, k, to):
+        return pltpu.make_async_remote_copy(
+            src_ref=src, dst_ref=dst, send_sem=sem.at[0, k], recv_sem=sem.at[1, k],
+            device_id={"row": to}, device_id_type=MESH,
+        )
+
+    gathered = (g_one, g_diag, g_top, g_zero)
+
+    def peer_copy(kind, m, slot):
+        buf = gathered[kind]
+        return pltpu.make_async_remote_copy(
+            src_ref=buf.at[slot], dst_ref=buf.at[slot],
+            send_sem=peer_send.at[kind, m], recv_sem=peer_recv.at[kind, m],
+            device_id={"col": (c + 2 * m) % n_col}, device_id_type=MESH,
+        )
+
+    def sib_copy(kind, m, slot):
+        buf = gathered[kind]
+        return pltpu.make_async_remote_copy(
+            src_ref=buf.at[slot], dst_ref=buf.at[slot],
+            send_sem=sib_send.at[kind, m], recv_sem=sib_recv.at[kind, m],
+            device_id={"col": sibling}, device_id_type=MESH,
+        )
+
+    def spread(kind):
+        for m in range(1, n_peer):
+            peer_copy(kind, m, c).start()
+        sib_copy(kind, 0, c).start()
+
+    def share(kind):
+        for m in range(1, n_peer):
+            slot = (c + n_col - 2 * m) % n_col
+            peer_copy(kind, m, slot).wait_recv()
+            sib_copy(kind, m, slot).start()
+
+    def settle(kind):
+        for m in range(n_peer):
+            sib_copy(kind, m, (sibling + n_col - 2 * m) % n_col).wait_recv()
+
+    spread(0)
+
+    diag_copy = hop(g_diag.at[c], g_diag.at[c], d_sem, 0, r + 1)
+
+    @pl.when(r > 0)
+    def _():
+        diag_copy.wait_recv()
+
+    @pl.when(r < n_row - 1)
+    def _():
+        diag_copy.start()
+
+    spread(1)
+
+    first = piv_ref[0:1, :].astype(F32)
+    second = piv_ref[1:2, :].astype(F32)
+    sub, lane = iota((PW, PW), 0).astype(F32), iota((PW, PW), 1).astype(F32)
+    eye = sub == lane
+
+    def upright(v):
+        return jnp.sum(jnp.where(eye, v, 0.0), axis=1, keepdims=True)
+
+    first_c, second_c = upright(first), upright(second)
+    lane_row = lane[0:1, :]
+    sub_col = sub[:, 0:1]
+
+    def lookup(match, found, otherwise, axis):
+        hit = jnp.sum(one_hot(match), axis=axis, keepdims=True)
+        return jnp.sum(jnp.where(match, found, 0.0), axis=axis, keepdims=True) + jnp.where(hit > 0.5, 0.0, otherwise)
+
+    q_second = lookup(first_c == second, sub, second, 0)
+    q_second_c = lookup(second_c == first, lane, second_c, 1)
+    home = lookup(first_c == lane + PW, sub, lane_row + PW, 0)
+    home_c = lookup(first == sub + PW, lane, sub_col + PW, 1)
+    out_first = jnp.where(first < tops, first, lookup(second_c == first, home_c, lane_row, 0))
+    out_second = jnp.where(q_second < tops, q_second, home)
+    q = jnp.concatenate([first, q_second], 1)
+    q_c = jnp.concatenate([first_c, q_second_c], 0)
+    outward = jnp.concatenate([out_first, out_second], 1)
+
+    start_f = start.astype(F32)
+    local = jnp.where(is_first, outward, q - start_f)
+    local_one = jnp.where(is_first, lane_row + PW, second - start_f)
+    mine = (q >= start_f) & (q < start_f + rows)
+    before = q < start_f
+    mine_one = (second >= start_f) & (second < start_f + rows)
+    before_one = second < start_f
+
+    pick_one = one_hot(iota((rows, PW), 0).astype(F32) == local_one).astype(BF16)
+    own_top = dot_pick(zero_t, pick_one)
+
+    right_l = hop(vl_out, vl_in, vl_sem, 0, r + 1)
+    left_l = hop(sl_out, sl_in, sl_sem, 0, r - 1)
+
+    def go_right_l():
+        @pl.when(is_first)
+        def _():
+            vl_out[...] = own_top
+            right_l.start()
+
+        @pl.when(r > 0)
+        def _():
+            right_l.wait_recv()
+
+        @pl.when((r > 0) & (r < n_row - 1))
+        def _():
+            vl_out[...] = jnp.where(mine_one, own_top, vl_in[...])
+            right_l.start()
+
+    def go_left_l():
+        @pl.when(is_last)
+        def _():
+            sl_out[...] = jnp.where(mine_one, own_top, 0.0)
+            left_l.start()
+
+        @pl.when(r < n_row - 1)
+        def _():
+            left_l.wait_recv()
+
+        @pl.when((r > 0) & (r < n_row - 1))
+        def _():
+            sl_out[...] = jnp.where(mine_one, own_top, sl_in[...])
+            left_l.start()
+
+    pick = one_hot(iota((rows, tops), 0).astype(F32) == local).astype(BF16)
+    own = dot_pick(block_t, pick)
+    part = cols // CHUNKS
+
+    def go_right(k):
+        at = pl.ds(k * part, part)
+        piece = own[k * part : (k + 1) * part]
+        copy = hop(v_out.at[at], v_in.at[at], v_sem, k, r + 1)
+
+        @pl.when(is_first)
+        def _():
+            v_out[at, :] = piece
+            copy.start()
+
+        @pl.when(r > 0)
+        def _():
+            copy.wait_recv()
+
+        @pl.when((r > 0) & (r < n_row - 1))
+        def _():
+            v_out[at, :] = jnp.where(mine, piece, v_in[at, :])
+            copy.start()
+
+    def go_left(k):
+        at = pl.ds(k * part, part)
+        piece = own[k * part : (k + 1) * part]
+        copy = hop(s_out.at[at], s_in.at[at], s_sem, k, r - 1)
+
+        @pl.when(is_last)
+        def _():
+            s_out[at, :] = jnp.where(mine, piece, 0.0)
+            copy.start()
+
+        @pl.when(r < n_row - 1)
+        def _():
+            copy.wait_recv()
+
+        @pl.when((r > 0) & (r < n_row - 1))
+        def _():
+            s_out[at, :] = jnp.where(mine, piece, s_in[at, :])
+            copy.start()
+
+    def both(right, left):
+        @pl.when(2 * r < n_row)
+        def _():
+            right()
+            left()
+
+        @pl.when(2 * r >= n_row)
+        def _():
+            left()
+            right()
+
+    both(go_right_l, go_left_l)
+
+    @pl.when(is_first)
+    def _():
+        g_top[c] = jnp.where(mine_one, own_top, sl_in[...])
+        g_zero[c] = zero_t
+
+    @pl.when(is_last)
+    def _():
+        g_top[c] = jnp.where(before_one, vl_in[...], own_top)
+
+    @pl.when((r > 0) & (r < n_row - 1))
+    def _():
+        g_top[c] = jnp.where(before_one, vl_in[...], jnp.where(mine_one, own_top, sl_in[...]))
+
+    @pl.when(r > 0)
+    def _():
+        put = one_hot(iota((PW, rows), 1).astype(F32) == second_c - start_f)
+        moved = jnp.sum(put, axis=0, keepdims=True) > 0.5
+        g_zero[c] = jnp.where(moved, dot_pick(vl_in[...], put.astype(BF16)), zero_t)
+
+    spread(2)
+    spread(3)
+
+    for k in range(CHUNKS):
+        both(lambda: go_right(k), lambda: go_left(k))
+        share(k)
+    settle(1)
+    inverses = [split(invert_upper(g_diag[:, p].reshape(PW, PW))) for p in range(2)]
+
+    for kind in (0, 2, 3):
+        settle(kind)
+
+    @pl.when(is_first)
+    def _():
+        v_in[...] = jnp.where(mine, own, s_in[...])
+
+    @pl.when(is_last)
+    def _():
+        s_in[...] = jnp.where(before, v_in[...], own)
+
+    @pl.when((r > 0) & (r < n_row - 1))
+    def _():
+        s_in[...] = jnp.where(before, v_in[...], jnp.where(mine, own, s_in[...]))
+
+    top = jnp.where(is_first, v_in[...], s_in[...])
+    upper0 = split(dot_split(split(top[:, :PW]), inverses[0]))
+    rest = top[:, PW:] - dot_split(upper0, split(g_top[...].reshape(PW, PW)))
+    upper1_full = dot_split(split(rest), inverses[1])
+    upper1 = split(upper1_full)
+
+    @pl.when(is_first)
+    def _():
+        upper0_full = dot_split(split(top[:, :PW]), inverses[0])
+        out_ref[...] = jnp.concatenate([upper0_full, upper1_full], 1).T
+
+    @pl.when(r > 0)
+    def _():
+        put = one_hot(iota((tops, rows), 1).astype(F32) == q_c - start_f)
+        moved = jnp.sum(put, axis=0, keepdims=True) > 0.5
+        work = jnp.where(moved, dot_pick(v_in[...], put.astype(BF16)), block_t)
+        work = work - dot_split(upper0, split(g_zero[...].reshape(PW, rows)))
+        work = work - dot_split(upper1, split(g_one[...].reshape(PW, rows)))
+        out_ref[...] = work.T
+
+    for kind in range(4):
+        for m in range(1, n_peer):
+            peer_copy(kind, m, c).wait_send()
+        for m in range(n_peer):
+            sib_copy(kind, m, c).wait_send()
+
+    @pl.when(r < n_row - 1)
+    def _():
+        diag_copy.wait_send()
+        right_l.wait_send()
+        for k in range(CHUNKS):
+            at = pl.ds(k * part, part)
+            hop(v_out.at[at], v_in.at[at], v_sem, k, r + 1).wait_send()
+
+    @pl.when(r > 0)
+    def _():
+        left_l.wait_send()
+        for k in range(CHUNKS):
+            at = pl.ds(k * part, part)
+            hop(s_out.at[at], s_in.at[at], s_sem, k, r - 1).wait_send()
+
+
+def fused(block, panels, pivots):
+    n_row, n_col = lax.axis_size("row"), lax.axis_size("col")
+    rows, cols = block.shape
+    kc = panels.shape[2]
+    tops = 2 * PW
+    vmem = pl.BlockSpec(memory_space=pltpu.VMEM)
+    n_peer = n_col // 2
+    dma = pltpu.SemaphoreType.DMA
+    return pl.pallas_call(
+        functools.partial(kernel, n_row, n_col),
+        out_shape=jax.ShapeDtypeStruct((rows, cols), F32),
+        in_specs=[vmem] * 3,
+        out_specs=vmem,
+        scratch_shapes=[
+            pltpu.VMEM((n_col, 2, kc, PW), F32),
+            pltpu.VMEM((n_col, kc, PW), F32),
+            pltpu.VMEM((n_col, kc, rows), F32),
+            pltpu.VMEM((n_col, kc, rows), F32),
+        ]
+        + [pltpu.VMEM((cols, tops), F32)] * 4
+        + [pltpu.VMEM((kc, PW), F32)] * 4
+        + [dma((2, 1))] * 3
+        + [dma((2, CHUNKS))] * 2
+        + [dma((4, n_peer))] * 4,
+        compiler_params=pltpu.CompilerParams(
+            collective_id=0, has_side_effects=True, vmem_limit_bytes=48 * 1024 * 1024
+        ),
+    )(pivots, block, panels)
+
+
+def body(block, panels, pivots):
+    fits = (
+        block.shape[0] == 2 * PW
+        and block.shape[1] % 128 == 0
+        and panels.shape[2] % 8 == 0
+        and lax.axis_size("col") % 2 == 0
+        and lax.axis_size("row") > 1
+    )
+    return fused(block, panels, pivots) if fits else plain(block, panels, pivots)
+
 
 def solution(mesh):
     return jax.shard_map(

time: 149 us -> 73.4 us (0.49)
  waiting for transfers between devices: 83.4 us -> 0 us
  Pallas kernels: 0 us -> 71.4 us
  local copies, waits for them, and re-layouts: 30.2 us -> 1.85 us
  matrix products: 15.7 us -> 0 us
  between operations: 13.7 us -> 0.03 us
  other arithmetic: 5.41 us -> 0 us
    psum x2 -> x0, waiting for transfers between devices: 74.6 us -> none  [body(): moved, diag_all = lax.psum((picked, diag_rows), 'row')]
    pallas_call x0 -> x1, Pallas kernels: none -> 71.4 us  [fused(): pl.pallas_call(functools.partial(kernel, n_row, n_col), out_shape=jax.Sha...]
    dot_general x32 -> x0, matrix products: 15.7 us -> none  [the longest x14 7.7 us: solve_top(): jnp.dot(power, power, precision=lax.Precision.HIGHEST, preferred_element_...]
    gather x8 -> x0, local copies, waits for them, and re-layouts: 13.7 us -> none  [the longest x4 9.73 us: pick_rows(): local_src = perm[targets] - start]
    scatter x6 -> x0, local copies, waits for them, and re-layouts: 9.55 us -> none  [the longest x4 5.68 us: swap_order(): return base.at[own].set(piv_row).at[piv_row].set(own)]
    all_gather x1 -> x0, waiting for transfers between devices: 8.74 us -> none  [body(): lowers = lax.all_gather(panels, 'col', axis=2, tiled=True)]
    select_n x10 -> x0, other arithmetic: 5.3 us -> none  [the longest x4 3.48 us: pick_rows(): return jnp.where(owned[:, None], taken, 0.0)]
    unnamed x16 -> x6, local copies, waits for them, and re-layouts: 4.46 us -> 1.85 us
  transfers between devices with their start and end apart: 3 -> 0, of which waited for: 3 -> 0; matrix products, arithmetic and copies ran while one was open for 13% -> 0% of each run, Pallas kernels for 0% -> 0%
where the time goes in v1:
time: 73.4 us; the launch traced here: 73.2 us
  Pallas kernels  71.4 us (97%)
  local copies, waits for them, and re-layouts  1.85 us (3%)
    pallas_call x1, Pallas kernels, fused(): pl.pallas_call(functools.partial(kernel, n_row, n_col), out_shape=jax.Sha...  71.4 us
    unnamed x6, local copies, waits for them, and re-layouts  1.85 us

profile of v1, /device:TPU:0, one launch (start us, length us, event | category | flops | bytes accessed | tf_op | source)
XLA Modules:
  0.0 73.2 jit_solution(7287532391615973500)
XLA Ops:
  0.0 0.0 copy-start.1
  0.0 0.0 copy-start
  0.0 1.1 %copy.4.panels_ref = f32[2,512,32]{2,1,0:T(8,128)S(1)} copy(f32[2,512,32]{1,2,0:T(8,128)} %param.4) | data formatting | bytes 262144 | tf_op args[1]
  1.2 0.0 copy-done.1
  1.2 0.0 copy-done
  1.2 71.4 %shard_map.37 = f32[512,128]{1,0:T(8,128)S(1)} custom-call(s32[2,256]{1,0:T(2,128)S(1)} %copy-done.1, f32[512,128]{1,0:T(8,128)S(1)} %copy-done, f32[2,512,32]{2,1,0:T(8,128)S(1)} %copy.4.panels_ref), custom_call_target="tpu_custom_call" | custom-call | tf_op jit(solution)/shard_map/pallas_call | solution.py:459
  72.5 0.7 copy.6
Async XLA Ops:
  0.0 1.2 %copy-start.1 = (s32[2,256]{1,0:T(2,128)S(1)}, s32[2,256]{1,0:T(2,128)}, u32[]{:S(2)}) copy-start(s32[2,256]{1,0:T(2,128)} %piv_ref.1) | copy-start | bytes 6148
  0.0 1.2 %copy-start = (f32[512,128]{1,0:T(8,128)S(1)}, f32[512,128]{1,0:T(8,128)}, u32[]{:S(2)}) copy-start(f32[512,128]{1,0:T(8,128)} %block_ref.1) | copy-start | bytes 786436

commit v2 on v0

--- a/solution.py
+++ b/solution.py
@@ -1,6 +1,10 @@
+import functools
+
 import jax
 import jax.numpy as jnp
 from jax import lax
+from jax.experimental import pallas as pl
+from jax.experimental.pallas import tpu as pltpu
 from jax.sharding import PartitionSpec as P
 
 PW = 256
@@ -53,7 +57,7 @@
     return jnp.where(in_top[:, None], placed, work)
 
 
-def body(block, panels, pivots):
+def plain(block, panels, pivots):
     rows_here = block.shape[0]
     rows_all = rows_here * lax.axis_size("row")
     start = lax.axis_index("row") * rows_here
@@ -76,6 +80,432 @@
         work = finish(work, lowers[panel], offset, start, upper)
     return work
 
+MESH = pl.DeviceIdType.MESH
+F32, BF16 = jnp.float32, jnp.bfloat16
+SMALL = 32
+DIAG, ONE, ZERO, TOP = range(4)
+
+
+def dot(a, b):
+    return jnp.dot(a, b, preferred_element_type=F32)
+
+
+def split(a):
+    high = a.astype(BF16)
+    return high, (a - high.astype(F32)).astype(BF16)
+
+
+def dot_split(a, b):
+    m = a[0].shape[0]
+    both = dot(jnp.concatenate(a, 0), b[0])
+    return both[:m] + (both[m:] + dot(a[0], b[1]))
+
+
+def dot_pick(a, one_hot):
+    m = a.shape[0]
+    high = a.astype(BF16)
+    rest = a - high.astype(F32)
+    mid = rest.astype(BF16)
+    low = (rest - mid.astype(F32)).astype(BF16)
+    out = dot(jnp.concatenate([high, mid, low], 0), one_hot)
+    return out[:m] + (out[m : 2 * m] + out[2 * m :])
+
+
+def iota(shape, dim):
+    return lax.broadcasted_iota(jnp.int32, shape, dim)
+
+
+def one_hot(condition):
+    return jnp.where(condition, 1.0, 0.0)
+
+
+def kernel(
+    n_row, n_col, piv_ref, block_ref, panels_ref, out_ref,
+    g, g_top, own_ref, f_in, f_out, l_in, l_out, power_ref, small_ref, inverse_ref,
+    d_sem, l_sem, f_sem, peer_send, peer_recv, sib_send, sib_recv,
+):
+    r, c = lax.axis_index("row"), lax.axis_index("col")
+    rows, cols = block_ref.shape
+    tops = 2 * PW
+    kc = panels_ref.shape[1]
+    n_peer = n_col // 2
+    chunks = cols // kc
+    last = n_row - 1
+    sibling = c + 1 - 2 * (c % 2)
+    is_first, is_last = r == 0, r == last
+    is_middle = (r > 0) & (r < last)
+    is_upper = 2 * r >= n_row
+    start = r * rows
+
+    barrier = pltpu.get_barrier_semaphore()
+
+    @pl.when(r > 0)
+    def _():
+        pl.semaphore_signal(barrier, 1, device_id={"row": r - 1}, device_id_type=MESH)
+
+    @pl.when(r < last)
+    def _():
+        pl.semaphore_signal(barrier, 1, device_id={"row": r + 1}, device_id_type=MESH)
+
+    for m in range(1, n_peer):
+        pl.semaphore_signal(barrier, 1, device_id={"col": (c + 2 * m) % n_col}, device_id_type=MESH)
+    pl.semaphore_signal(barrier, 1, device_id={"col": sibling}, device_id_type=MESH)
+
+    first = piv_ref[0:1, :].astype(F32)
+    second = piv_ref[1:2, :].astype(F32)
+    sub, lane = iota((PW, PW), 0).astype(F32), iota((PW, PW), 1).astype(F32)
+
+    def upright(v):
+        return jnp.sum(jnp.where(sub == lane, v, 0.0), axis=1, keepdims=True)
+
+    first_c, second_c = upright(first), upright(second)
+    lane_row = lane[0:1, :]
+    sub_col = sub[:, 0:1]
+
+    def lookup(match, found, otherwise, axis):
+        hit = jnp.sum(one_hot(match), axis=axis, keepdims=True)
+        return jnp.sum(jnp.where(match, found, 0.0), axis=axis, keepdims=True) + jnp.where(hit > 0.5, 0.0, otherwise)
+
+    q_second = lookup(first_c == second, sub, second, 0)
+    q_second_c = lookup(second_c == first, lane, second_c, 1)
+    home = lookup(first_c == lane + PW, sub, lane_row + PW, 0)
+    home_c = lookup(first == sub + PW, lane, sub_col + PW, 1)
+    out_first = jnp.where(first < tops, first, lookup(second_c == first, home_c, lane_row, 0))
+    out_second = jnp.where(q_second < tops, q_second, home)
+    q = jnp.concatenate([first, q_second], 1)
+    q_c = jnp.concatenate([first_c, q_second_c], 0)
+    outward = jnp.concatenate([out_first, out_second], 1)
+
+    start_f = start.astype(F32)
+    local = jnp.where(is_first, outward, q - start_f)
+    local_one = jnp.where(is_first, lane_row + PW, second - start_f)
+
+    def from_here(v):
+        return (v >= start_f) & (v < start_f + rows)
+
+    own_top = dot_pick(panels_ref[0], one_hot(iota((rows, PW), 0).astype(F32) == local_one).astype(BF16))
+    l_out[0] = own_top
+    l_out[1] = own_top
+    block_t = block_ref[...].T
+    own = dot_pick(block_t, one_hot(iota((rows, tops), 0).astype(F32) == local).astype(BF16))
+    own_ref[...] = own
+    f_out[0] = own
+    f_out[1] = own
+
+    @pl.when(is_first)
+    def _():
+        g[DIAG, c] = jnp.concatenate([panels_ref[0, :, :PW], panels_ref[1, :, PW:tops]], 1)
+
+    @pl.when(r > 0)
+    def _():
+        g[ONE, c] = panels_ref[1]
+
+    @pl.when(is_middle)
+    def _():
+        pl.semaphore_wait(barrier, n_peer + 2)
+
+    @pl.when(is_first | is_last)
+    def _():
+        pl.semaphore_wait(barrier, n_peer + 1)
+
+    def l_copy(d):
+        return pltpu.make_async_remote_copy(
+            src_ref=l_out.at[d], dst_ref=l_in.at[d], send_sem=l_sem.at[0, d], recv_sem=l_sem.at[1, d],
+            device_id={"row": r + 1 - 2 * d}, device_id_type=MESH,
+        )
+
+    def f_copy(k, d):
+        at = pl.ds(pl.multiple_of(k * kc, 8), kc)
+        return pltpu.make_async_remote_copy(
+            src_ref=f_out.at[d, at], dst_ref=f_in.at[d, at],
+            send_sem=f_sem.at[0, d, k], recv_sem=f_sem.at[1, d, k],
+            device_id={"row": r + 1 - 2 * d}, device_id_type=MESH,
+        )
+
+    diag_copy = pltpu.make_async_remote_copy(
+        src_ref=g.at[DIAG, c], dst_ref=g.at[DIAG, c], send_sem=d_sem.at[0], recv_sem=d_sem.at[1],
+        device_id={"row": r + 1}, device_id_type=MESH,
+    )
+
+    def arrives(d):
+        return jnp.where(d == 0, r > 0, r < last)
+
+    def l_step(d):
+        @pl.when(arrives(d))
+        def _():
+            l_copy(d).wait_recv()
+
+        @pl.when(is_middle)
+        def _():
+            l_out[d] = jnp.where(from_here(second), l_out[d], l_in[d])
+            l_copy(d).start()
+
+    def f_step(k, d):
+        @pl.when(arrives(d))
+        def _():
+            f_copy(k, d).wait_recv()
+
+        @pl.when(is_middle)
+        def _():
+            at = pl.ds(pl.multiple_of(k * kc, 8), kc)
+            f_out[d, at, :] = jnp.where(from_here(q), f_out[d, at, :], f_in[d, at, :])
+            f_copy(k, d).start()
+
+    def slot_ref(kind, slot):
+        return g_top.at[slot] if kind == TOP else g.at[kind, slot]
+
+    def peer_copy(kind, m, slot):
+        return pltpu.make_async_remote_copy(
+            src_ref=slot_ref(kind, slot), dst_ref=slot_ref(kind, slot),
+            send_sem=peer_send.at[kind, m], recv_sem=peer_recv.at[kind, m],
+            device_id={"col": (c + 2 * m) % n_col}, device_id_type=MESH,
+        )
+
+    def sib_copy(kind, m, slot):
+        return pltpu.make_async_remote_copy(
+            src_ref=slot_ref(kind, slot), dst_ref=slot_ref(kind, slot),
+            send_sem=sib_send.at[kind, m], recv_sem=sib_recv.at[kind, m],
+            device_id={"col": sibling}, device_id_type=MESH,
+        )
+
+    def spread(kind):
+        for m in range(1, n_peer):
+            peer_copy(kind, m, c).start()
+        sib_copy(kind, 0, c).start()
+
+    def share(kind):
+        for m in range(1, n_peer):
+            slot = (c + n_col - 2 * m) % n_col
+            peer_copy(kind, m, slot).wait_recv()
+            sib_copy(kind, m, slot).start()
+
+    def settle(kind):
+        for m in range(n_peer):
+            sib_copy(kind, m, (sibling + n_col - 2 * m) % n_col).wait_recv()
+
+    def drain(kind):
+        for m in range(1, n_peer):
+            peer_copy(kind, m, c).wait_send()
+        for m in range(n_peer):
+            sib_copy(kind, m, c).wait_send()
+
+    @pl.when(is_first)
+    def _():
+        diag_copy.start()
+        spread(DIAG)
+        l_copy(0).start()
+        for k in range(chunks):
+            f_copy(k, 0).start()
+
+    @pl.when(is_last)
+    def _():
+        l_copy(1).start()
+        for k in range(chunks):
+            f_copy(k, 1).start()
+
+    @pl.when(is_upper)
+    def _():
+        l_step(1)
+
+    @pl.when(r > 0)
+    def _():
+        diag_copy.wait_recv()
+
+        @pl.when(r < last)
+        def _():
+            diag_copy.start()
+
+        spread(DIAG)
+
+    l_step(0)
+
+    @pl.when(jnp.logical_not(is_upper))
+    def _():
+        l_step(1)
+
+    top_rows = jnp.where(second < start_f, l_in[0], jnp.where(from_here(second), own_top, l_in[1]))
+    g_top[c] = top_rows
+    spread(TOP)
+
+    @pl.when(r > 0)
+    def _():
+        put = one_hot(iota((PW, rows), 1).astype(F32) == second_c - start_f)
+        moved = jnp.sum(put, axis=0, keepdims=True) > 0.5
+        g[ZERO, c] = jnp.where(moved, dot_pick(l_in[0], put.astype(BF16)), panels_ref[0])
+        spread(ZERO)
+        spread(ONE)
+
+    def strict(p):
+        upper = g[DIAG, :, :, p * PW : (p + 1) * PW].reshape(PW, PW)
+        return jnp.where(iota((PW, PW), 0) < iota((PW, PW), 1), upper, 0.0)
+
+    def spaced(small):
+        same = iota((PW, PW), 0) // SMALL == iota((PW, PW), 1) // SMALL
+        return jnp.where(same, jnp.concatenate([small] * (PW // SMALL), 0), 0.0)
+
+    def begin():
+        share(DIAG)
+        settle(DIAG)
+        lanes = iota((SMALL, PW), 1)
+        for p in range(2):
+            whole = strict(p)
+            small = jnp.zeros((SMALL, PW), F32)
+            for b in range(PW // SMALL):
+                small += jnp.where(lanes // SMALL == b, whole[b * SMALL : (b + 1) * SMALL], 0.0)
+            small_ref[p] = one_hot(lanes % SMALL == iota((SMALL, PW), 0)) - small
+            power_ref[p] = dot_split(split(small), split(spaced(small)))
+
+    def double(_, carry):
+        for p in range(2):
+            power, small = power_ref[p], small_ref[p]
+            new = dot_split(split(jnp.concatenate([power, small], 0)), split(spaced(power)))
+            power_ref[p] = new[:SMALL]
+            small_ref[p] = small + new[SMALL:]
+        return carry
+
+    def widen():
+        for p in range(2):
+            inverse_ref[p] = spaced(small_ref[p])
+
+    def merge(level):
+        shift = SMALL.bit_length() - 1 + level
+        row, col = iota((PW, PW), 0), iota((PW, PW), 1)
+        pair = ((row >> (shift + 1)) == (col >> (shift + 1))) & ((row >> shift) != (col >> shift))
+        for p in range(2):
+            inverse = inverse_ref[p]
+            parts = split(inverse)
+            right = dot_split(split(jnp.where(pair, strict(p), 0.0)), parts)
+            inverse_ref[p] = inverse - dot_split(parts, split(right))
+
+    doublings = SMALL.bit_length() - 2
+    merges = (PW // SMALL).bit_length() - 1
+
+    def turn(k, carry):
+        @pl.when(k < chunks)
+        def _():
+            upper = jnp.where(is_upper, 1, 0)
+            f_step(k, upper)
+            f_step(k, 1 - upper)
+
+        @pl.when(k == 0)
+        def _():
+            begin()
+
+        @pl.when(k == 1)
+        def _():
+            share(TOP)
+
+        @pl.when((k == 2) & (r > 0))
+        def _():
+            share(ZERO)
+
+        @pl.when((k == 3) & (r > 0))
+        def _():
+            share(ONE)
+
+        @pl.when(k < 2)
+        def _():
+            lax.fori_loop(0, doublings // 2, double, 0)
+
+        @pl.when(k == 2)
+        def _():
+            widen()
+
+        @pl.when(k >= 2)
+        def _():
+            merge(k - 2)
+
+        return carry
+
+    lax.fori_loop(0, 2 + merges, turn, 0)
+    settle(TOP)
+
+    top = jnp.where(q < start_f, f_in[0], jnp.where(from_here(q), own_ref[...], f_in[1]))
+    upper0_full = dot_split(split(top[:, :PW]), split(inverse_ref[0]))
+    upper0 = split(upper0_full)
+    rest = top[:, PW:] - dot_split(upper0, split(g_top[...].reshape(PW, PW)))
+    upper1_full = dot_split(split(rest), split(inverse_ref[1]))
+
+    @pl.when(is_first)
+    def _():
+        out_ref[...] = jnp.concatenate([upper0_full, upper1_full], 1).T
+
+    @pl.when(r > 0)
+    def _():
+        settle(ZERO)
+        settle(ONE)
+        put = one_hot(iota((tops, rows), 1).astype(F32) == q_c - start_f)
+        moved = jnp.sum(put, axis=0, keepdims=True) > 0.5
+        work = jnp.where(moved, dot_pick(f_in[0], put.astype(BF16)), block_ref[...].T)
+        work = work - dot_split(upper0, split(g[ZERO].reshape(PW, rows)))
+        work = work - dot_split(split(upper1_full), split(g[ONE].reshape(PW, rows)))
+        out_ref[...] = work.T
+        drain(ZERO)
+        drain(ONE)
+
+    drain(DIAG)
+    drain(TOP)
+
+    @pl.when(r < last)
+    def _():
+        diag_copy.wait_send()
+
+    for d in range(2):
+        @pl.when((r < last) if d == 0 else (r > 0))
+        def _():
+            l_copy(d).wait_send()
+            for k in range(chunks):
+                f_copy(k, d).wait_send()
+
+
+def fused(block, panels, pivots):
+    n_row, n_col = lax.axis_size("row"), lax.axis_size("col")
+    rows, cols = block.shape
+    kc = panels.shape[2]
+    tops = 2 * PW
+    vmem = pl.BlockSpec(memory_space=pltpu.VMEM)
+    n_peer = n_col // 2
+    dma = pltpu.SemaphoreType.DMA
+    return pl.pallas_call(
+        functools.partial(kernel, n_row, n_col),
+        out_shape=jax.ShapeDtypeStruct((rows, cols), F32),
+        in_specs=[vmem] * 3,
+        out_specs=vmem,
+        scratch_shapes=[
+            pltpu.VMEM((3, n_col, kc, rows), F32),
+            pltpu.VMEM((n_col, kc, PW), F32),
+            pltpu.VMEM((cols, tops), F32),
+            pltpu.VMEM((2, cols, tops), F32),
+            pltpu.VMEM((2, cols, tops), F32),
+            pltpu.VMEM((2, kc, PW), F32),
+            pltpu.VMEM((2, kc, PW), F32),
+            pltpu.VMEM((2, SMALL, PW), F32),
+            pltpu.VMEM((2, SMALL, PW), F32),
+            pltpu.VMEM((2, PW, PW), F32),
+            dma((2,)),
+            dma((2, 2)),
+            dma((2, 2, cols // kc)),
+        ]
+        + [dma((4, n_peer))] * 4,
+        compiler_params=pltpu.CompilerParams(
+            collective_id=0, has_side_effects=True, vmem_limit_bytes=48 * 1024 * 1024
+        ),
+    )(pivots, block, jnp.swapaxes(panels, 1, 2))
+
+
+def body(block, panels, pivots):
+    kc = panels.shape[2]
+    fits = (
+        block.shape[0] == 2 * PW
+        and block.shape[1] % 128 == 0
+        and kc % 8 == 0
+        and block.shape[1] // kc in range(1, 6)
+        and block.shape[1] % kc == 0
+        and lax.axis_size("col") % 2 == 0
+        and lax.axis_size("row") > 1
+    )
+    return fused(block, panels, pivots) if fits else plain(block, panels, pivots)
+
 
 def solution(mesh):
     return jax.shard_map(

time: 149 us -> 39 us (0.26)
  waiting for transfers between devices: 83.4 us -> 0 us
  Pallas kernels: 0 us -> 35.5 us
  local copies, waits for them, and re-layouts: 30.2 us -> 3.24 us
  matrix products: 15.7 us -> 0 us
  between operations: 13.7 us -> 0.01 us
  other arithmetic: 5.41 us -> 0 us
    psum x2 -> x0, waiting for transfers between devices: 74.6 us -> none  [body(): moved, diag_all = lax.psum((picked, diag_rows), 'row')]
    pallas_call x0 -> x1, Pallas kernels: none -> 35.5 us  [fused(): pl.pallas_call(functools.partial(kernel, n_row, n_col), out_shape=jax.Sha...]
    dot_general x32 -> x0, matrix products: 15.7 us -> none  [the longest x14 7.7 us: solve_top(): jnp.dot(power, power, precision=lax.Precision.HIGHEST, preferred_element_...]
    gather x8 -> x0, local copies, waits for them, and re-layouts: 13.7 us -> none  [the longest x4 9.73 us: pick_rows(): local_src = perm[targets] - start]
    scatter x6 -> x0, local copies, waits for them, and re-layouts: 9.55 us -> none  [the longest x4 5.68 us: swap_order(): return base.at[own].set(piv_row).at[piv_row].set(own)]
    all_gather x1 -> x0, waiting for transfers between devices: 8.74 us -> none  [body(): lowers = lax.all_gather(panels, 'col', axis=2, tiled=True)]
    select_n x10 -> x0, other arithmetic: 5.3 us -> none  [the longest x4 3.48 us: pick_rows(): return jnp.where(owned[:, None], taken, 0.0)]
    slice x2 -> x0, local copies, waits for them, and re-layouts: 2.47 us -> none  [the longest x1 2.46 us: body(): work = finish(work, lowers[panel], offset, start, upper)]
  transfers between devices with their start and end apart: 3 -> 0, of which waited for: 3 -> 0; matrix products, arithmetic and copies ran while one was open for 13% -> 0% of each run, Pallas kernels for 0% -> 0%
where the time goes in v2:
time: 39 us; the launch traced here: 38.8 us
  Pallas kernels  35.5 us (91%)
  local copies, waits for them, and re-layouts  3.24 us (8%)
    pallas_call x1, Pallas kernels, fused(): pl.pallas_call(functools.partial(kernel, n_row, n_col), out_shape=jax.Sha...  35.5 us
    unnamed x7, local copies, waits for them, and re-layouts  3.24 us

profile of v2, /device:TPU:0, one launch (start us, length us, event | category | flops | bytes accessed | tf_op | source)
XLA Modules:
  0.0 38.8 jit_solution(1796967924540281028)
XLA Ops:
  0.0 0.0 copy-start
  0.0 0.9 %copy-done = f32[512,128]{1,0:T(8,128)S(1)} copy-done((f32[512,128]{1,0:T(8,128)S(1)}, f32[512,128]{1,0:T(8,128)}, u32[]{:S(2)}) %copy-start) | copy-done | bytes 262168
  1.0 0.0 copy-start.1
  1.0 0.9 %copy-done.1 = f32[2,512,32]{1,2,0:T(8,128)S(1)} copy-done((f32[2,512,32]{1,2,0:T(8,128)S(1)}, f32[2,512,32]{1,2,0:T(8,128)}, u32[]{:S(2)}) %copy-start.1) | copy-done | bytes 131096
  1.9 0.0 copy-start.2
  1.9 0.7 %copy-done.2 = s32[2,256]{1,0:T(2,128)S(1)} copy-done((s32[2,256]{1,0:T(2,128)S(1)}, s32[2,256]{1,0:T(2,128)}, u32[]{:S(2)}) %copy-start.2) | copy-done | bytes 2072
  2.5 35.5 %shard_map.37 = f32[512,128]{1,0:T(8,128)S(1)} custom-call(s32[2,256]{1,0:T(2,128)S(1)} %copy-done.2, f32[512,128]{1,0:T(8,128)S(1)} %copy-done, f32[2,32,512]{2,1,0:T(8,128)S(1)} %bitcast.1), custom_call_target="tpu_custom_call" | custom-call | tf_op jit(solution)/shard_map/pallas_call | solution.py:469
  38.1 0.7 %copy.5 = f32[512,128]{1,0:T(8,128)} copy(f32[512,128]{1,0:T(8,128)S(1)} %shard_map.37) | data formatting | bytes 524288
Async XLA Ops:
  0.0 0.9 %copy-start = (f32[512,128]{1,0:T(8,128)S(1)}, f32[512,128]{1,0:T(8,128)}, u32[]{:S(2)}) copy-start(f32[512,128]{1,0:T(8,128)} %block_ref.1) | copy-start | bytes 786436
  1.0 0.9 %copy-start.1 = (f32[2,512,32]{1,2,0:T(8,128)S(1)}, f32[2,512,32]{1,2,0:T(8,128)}, u32[]{:S(2)}) copy-start(f32[2,512,32]{1,2,0:T(8,128)} %param.4) | copy-start | bytes 393220
  1.9 0.7 %copy-start.2 = (s32[2,256]{1,0:T(2,128)S(1)}, s32[2,256]{1,0:T(2,128)}, u32[]{:S(2)}) copy-start(s32[2,256]{1,0:T(2,128)} %piv_ref.1) | copy-start | bytes 6148

commit v3 on v2

--- a/solution.py
+++ b/solution.py
@@ -101,13 +101,19 @@
     return both[:m] + (both[m:] + dot(a[0], b[1]))
 
 
-def dot_pick(a, one_hot):
+def three(parts_ref, a):
     m = a.shape[0]
     high = a.astype(BF16)
     rest = a - high.astype(F32)
     mid = rest.astype(BF16)
-    low = (rest - mid.astype(F32)).astype(BF16)
-    out = dot(jnp.concatenate([high, mid, low], 0), one_hot)
+    parts_ref[0:m] = high
+    parts_ref[m : 2 * m] = mid
+    parts_ref[2 * m : 3 * m] = (rest - mid.astype(F32)).astype(BF16)
+
+
+def pick(parts_ref, one_hot):
+    out = dot(parts_ref[...], one_hot.astype(BF16))
+    m = out.shape[0] // 3
     return out[:m] + (out[m : 2 * m] + out[2 * m :])
 
 
@@ -120,11 +126,21 @@
 
 
 def kernel(
-    n_row, n_col, piv_ref, block_ref, panels_ref, out_ref,
+    n_row, n_col, piv_hbm, block_hbm, panels_hbm, out_ref,
+    piv_ref, block_ref, panels_ref, block_t, load_sem,
     g, g_top, own_ref, f_in, f_out, l_in, l_out, power_ref, small_ref, inverse_ref,
+    own_top_ref, parts, parts_one, put_parts_one, index,
     d_sem, l_sem, f_sem, peer_send, peer_recv, sib_send, sib_recv,
 ):
     r, c = lax.axis_index("row"), lax.axis_index("col")
+    loads = [
+        pltpu.make_async_copy(src, dst, load_sem.at[i])
+        for i, (src, dst) in enumerate(
+            ((piv_hbm, piv_ref), (panels_hbm, panels_ref), (block_hbm, block_ref))
+        )
+    ]
+    for load in loads:
+        load.start()
     rows, cols = block_ref.shape
     tops = 2 * PW
     kc = panels_ref.shape[1]
@@ -151,6 +167,7 @@
         pl.semaphore_signal(barrier, 1, device_id={"col": (c + 2 * m) % n_col}, device_id_type=MESH)
     pl.semaphore_signal(barrier, 1, device_id={"col": sibling}, device_id_type=MESH)
 
+    loads[0].wait()
     first = piv_ref[0:1, :].astype(F32)
     second = piv_ref[1:2, :].astype(F32)
     sub, lane = iota((PW, PW), 0).astype(F32), iota((PW, PW), 1).astype(F32)
@@ -183,14 +200,34 @@
     def from_here(v):
         return (v >= start_f) & (v < start_f + rows)
 
-    own_top = dot_pick(panels_ref[0], one_hot(iota((rows, PW), 0).astype(F32) == local_one).astype(BF16))
-    l_out[0] = own_top
-    l_out[1] = own_top
-    block_t = block_ref[...].T
-    own = dot_pick(block_t, one_hot(iota((rows, tops), 0).astype(F32) == local).astype(BF16))
-    own_ref[...] = own
-    f_out[0] = own
-    f_out[1] = own
+    loads[1].wait()
+    loads[2].wait()
+    index[0:1, 0:tops] = local
+    index[0:1, tops : tops + PW] = local_one
+    for n in range(rows // 128):
+        block_t[:, n * 128 : (n + 1) * 128] = block_ref[n * 128 : (n + 1) * 128, :].T
+    three(parts, block_t[...])
+    three(parts_one, panels_ref[0])
+
+    def take(n, carry):
+        at = pl.ds(pl.multiple_of(n * 128, 128), 128)
+        picked = pick(parts, one_hot(iota((rows, 128), 0).astype(F32) == index[0:1, at]))
+        own_ref[:, at] = picked
+        f_out[0, :, at] = picked
+        f_out[1, :, at] = picked
+        return carry
+
+    def take_one(n, carry):
+        at = pl.ds(pl.multiple_of(n * 128, 128), 128)
+        here = pl.ds(pl.multiple_of(tops + n * 128, 128), 128)
+        picked = pick(parts_one, one_hot(iota((rows, 128), 0).astype(F32) == index[0:1, here]))
+        own_top_ref[:, at] = picked
+        l_out[0, :, at] = picked
+        l_out[1, :, at] = picked
+        return carry
+
+    lax.fori_loop(0, PW // 128, take_one, 0)
+    lax.fori_loop(0, tops // 128, take, 0)
 
     @pl.when(is_first)
     def _():
@@ -323,20 +360,27 @@
     def _():
         l_step(1)
 
-    top_rows = jnp.where(second < start_f, l_in[0], jnp.where(from_here(second), own_top, l_in[1]))
+    top_rows = jnp.where(second < start_f, l_in[0], jnp.where(from_here(second), own_top_ref[...], l_in[1]))
     g_top[c] = top_rows
     spread(TOP)
 
     @pl.when(r > 0)
     def _():
-        put = one_hot(iota((PW, rows), 1).astype(F32) == second_c - start_f)
-        moved = jnp.sum(put, axis=0, keepdims=True) > 0.5
-        g[ZERO, c] = jnp.where(moved, dot_pick(l_in[0], put.astype(BF16)), panels_ref[0])
+        three(put_parts_one, l_in[0])
+
+        def put_one(n, carry):
+            at = pl.ds(pl.multiple_of(n * 128, 128), 128)
+            put = one_hot((iota((PW, 128), 1) + n * 128).astype(F32) == second_c - start_f)
+            moved = jnp.sum(put, axis=0, keepdims=True) > 0.5
+            g[ZERO, c, :, at] = jnp.where(moved, pick(put_parts_one, put), panels_ref[0, :, at])
+            return carry
+
+        lax.fori_loop(0, rows // 128, put_one, 0)
         spread(ZERO)
         spread(ONE)
 
     def strict(p):
-        upper = g[DIAG, :, :, p * PW : (p + 1) * PW].reshape(PW, PW)
+        upper = g[DIAG, :, :, pl.ds(pl.multiple_of(p * PW, 128), PW)].reshape(PW, PW)
         return jnp.where(iota((PW, PW), 0) < iota((PW, PW), 1), upper, 0.0)
 
     def spaced(small):
@@ -347,21 +391,26 @@
         share(DIAG)
         settle(DIAG)
         lanes = iota((SMALL, PW), 1)
-        for p in range(2):
+        def one(p, carry):
             whole = strict(p)
             small = jnp.zeros((SMALL, PW), F32)
             for b in range(PW // SMALL):
                 small += jnp.where(lanes // SMALL == b, whole[b * SMALL : (b + 1) * SMALL], 0.0)
             small_ref[p] = one_hot(lanes % SMALL == iota((SMALL, PW), 0)) - small
             power_ref[p] = dot_split(split(small), split(spaced(small)))
+            return carry
+
+        lax.fori_loop(0, 2, one, 0)
 
     def double(_, carry):
-        for p in range(2):
+        def one(p, carry):
             power, small = power_ref[p], small_ref[p]
             new = dot_split(split(jnp.concatenate([power, small], 0)), split(spaced(power)))
             power_ref[p] = new[:SMALL]
             small_ref[p] = small + new[SMALL:]
-        return carry
+            return carry
+
+        return lax.fori_loop(0, 2, one, carry)
 
     def widen():
         for p in range(2):
@@ -371,11 +420,14 @@
         shift = SMALL.bit_length() - 1 + level
         row, col = iota((PW, PW), 0), iota((PW, PW), 1)
         pair = ((row >> (shift + 1)) == (col >> (shift + 1))) & ((row >> shift) != (col >> shift))
-        for p in range(2):
+        def one(p, carry):
             inverse = inverse_ref[p]
             parts = split(inverse)
             right = dot_split(split(jnp.where(pair, strict(p), 0.0)), parts)
             inverse_ref[p] = inverse - dot_split(parts, split(right))
+            return carry
+
+        lax.fori_loop(0, 2, one, 0)
 
     doublings = SMALL.bit_length() - 2
     merges = (PW // SMALL).bit_length() - 1
@@ -434,12 +486,20 @@
     def _():
         settle(ZERO)
         settle(ONE)
-        put = one_hot(iota((tops, rows), 1).astype(F32) == q_c - start_f)
-        moved = jnp.sum(put, axis=0, keepdims=True) > 0.5
-        work = jnp.where(moved, dot_pick(f_in[0], put.astype(BF16)), block_ref[...].T)
-        work = work - dot_split(upper0, split(g[ZERO].reshape(PW, rows)))
-        work = work - dot_split(split(upper1_full), split(g[ONE].reshape(PW, rows)))
-        out_ref[...] = work.T
+        three(parts, f_in[0])
+        both = jnp.concatenate([upper0_full, upper1_full], 1)
+        left = split(both)
+
+        def finish_rows(n, carry):
+            at = pl.ds(pl.multiple_of(n * 128, 128), 128)
+            put = one_hot((iota((tops, 128), 1) + n * 128).astype(F32) == q_c - start_f)
+            moved = jnp.sum(put, axis=0, keepdims=True) > 0.5
+            work = jnp.where(moved, pick(parts, put), block_t[:, at])
+            lower = jnp.concatenate([g[ZERO, :, :, at].reshape(PW, 128), g[ONE, :, :, at].reshape(PW, 128)], 0)
+            out_ref[at, :] = (work - dot_split(left, split(lower))).T
+            return carry
+
+        lax.fori_loop(0, rows // 128, finish_rows, 0)
         drain(ZERO)
         drain(ONE)
 
@@ -469,9 +529,14 @@
     return pl.pallas_call(
         functools.partial(kernel, n_row, n_col),
         out_shape=jax.ShapeDtypeStruct((rows, cols), F32),
-        in_specs=[vmem] * 3,
+        in_specs=[pl.BlockSpec(memory_space=pl.ANY)] * 3,
         out_specs=vmem,
         scratch_shapes=[
+            pltpu.VMEM(pivots.shape, jnp.int32),
+            pltpu.VMEM((rows, cols), F32),
+            pltpu.VMEM((2, kc, rows), F32),
+            pltpu.VMEM((cols, rows), F32),
+            dma((3,)),
             pltpu.VMEM((3, n_col, kc, rows), F32),
             pltpu.VMEM((n_col, kc, PW), F32),
             pltpu.VMEM((cols, tops), F32),
@@ -482,13 +547,18 @@
             pltpu.VMEM((2, SMALL, PW), F32),
             pltpu.VMEM((2, SMALL, PW), F32),
             pltpu.VMEM((2, PW, PW), F32),
+            pltpu.VMEM((kc, PW), F32),
+            pltpu.VMEM((3 * cols, tops), BF16),
+            pltpu.VMEM((3 * kc, rows), BF16),
+            pltpu.VMEM((3 * kc, PW), BF16),
+            pltpu.VMEM((8, tops + PW), F32),
             dma((2,)),
             dma((2, 2)),
             dma((2, 2, cols // kc)),
         ]
         + [dma((4, n_peer))] * 4,
         compiler_params=pltpu.CompilerParams(
-            collective_id=0, has_side_effects=True, vmem_limit_bytes=48 * 1024 * 1024
+            collective_id=0, has_side_effects=True, vmem_limit_bytes=60 * 1024 * 1024
         ),
     )(pivots, block, jnp.swapaxes(panels, 1, 2))
 

time: 39 us -> 41.7 us (1.069)
  Pallas kernels: 35.5 us -> 39.9 us
  local copies, waits for them, and re-layouts: 3.24 us -> 1.67 us
    pallas_call x1, Pallas kernels: 35.5 us -> 39.9 us  [fused(): pl.pallas_call(functools.partial(kernel, n_row, n_col), out_shape=jax.Sha...]
    unnamed x7 -> x1, local copies, waits for them, and re-layouts: 3.24 us -> 1.67 us
where the time goes in v3:
time: 41.7 us; the launch traced here: 41.5 us
  Pallas kernels  39.9 us (96%)
  local copies, waits for them, and re-layouts  1.67 us (4%)
    pallas_call x1, Pallas kernels, fused(): pl.pallas_call(functools.partial(kernel, n_row, n_col), out_shape=jax.Sha...  39.9 us
    unnamed x1, local copies, waits for them, and re-layouts  1.67 us

profile of v3, /device:TPU:0, one launch (start us, length us, event | category | flops | bytes accessed | tf_op | source)
XLA Modules:
  0.0 41.5 jit_solution(8349496604117212656)
XLA Ops:
  0.0 39.9 %shard_map.37 = f32[512,128]{1,0:T(8,128)} custom-call(s32[2,256]{1,0:T(2,128)} %piv_hbm.1, f32[512,128]{1,0:T(8,128)} %block_hbm.1, f32[2,32,512]{2,1,0:T(8,128)} %bitcast.1), custom_call_target="tpu_custom_call" | custom-call | tf_op jit(solution)/shard_map/pallas_call | solution.py:529
  39.9 1.7 %copy.5 = f32[512,128]{1,0:T(8,128)} copy(f32[512,128]{1,0:T(8,128)} %shard_map.37) | data formatting | bytes 524288

commit v4 on v2

--- a/solution.py
+++ b/solution.py
@@ -83,7 +83,7 @@
 MESH = pl.DeviceIdType.MESH
 F32, BF16 = jnp.float32, jnp.bfloat16
 SMALL = 32
-DIAG, ONE, ZERO, TOP = range(4)
+ONE, ZERO, TOP, DIAG = range(4)
 
 
 def dot(a, b):
@@ -120,9 +120,9 @@
 
 
 def kernel(
-    n_row, n_col, piv_ref, block_ref, panels_ref, out_ref,
-    g, g_top, own_ref, f_in, f_out, l_in, l_out, power_ref, small_ref, inverse_ref,
-    d_sem, l_sem, f_sem, peer_send, peer_recv, sib_send, sib_recv,
+    n_row, n_col, piv_ref, block_ref, panels_ref, out_ref, d_from, g_diag,
+    g, g_top, own_ref, f_in, f_out, l_in, l_out, inverse_ref,
+    d_sem, i_sem, l_sem, f_sem, peer_send, peer_recv, sib_send, sib_recv,
 ):
     r, c = lax.axis_index("row"), lax.axis_index("col")
     rows, cols = block_ref.shape
@@ -131,7 +131,8 @@
     n_peer = n_col // 2
     chunks = cols // kc
     last = n_row - 1
-    sibling = c + 1 - 2 * (c % 2)
+    p = c % 2
+    sibling = c + 1 - 2 * p
     is_first, is_last = r == 0, r == last
     is_middle = (r > 0) & (r < last)
     is_upper = 2 * r >= n_row
@@ -147,9 +148,8 @@
     def _():
         pl.semaphore_signal(barrier, 1, device_id={"row": r + 1}, device_id_type=MESH)
 
-    for m in range(1, n_peer):
-        pl.semaphore_signal(barrier, 1, device_id={"col": (c + 2 * m) % n_col}, device_id_type=MESH)
-    pl.semaphore_signal(barrier, 1, device_id={"col": sibling}, device_id_type=MESH)
+    for m in range(1, n_col):
+        pl.semaphore_signal(barrier, 1, device_id={"col": (c + m) % n_col}, device_id_type=MESH)
 
     first = piv_ref[0:1, :].astype(F32)
     second = piv_ref[1:2, :].astype(F32)
@@ -194,7 +194,8 @@
 
     @pl.when(is_first)
     def _():
-        g[DIAG, c] = jnp.concatenate([panels_ref[0, :, :PW], panels_ref[1, :, PW:tops]], 1)
+        d_from[0] = panels_ref[0, :, :PW]
+        d_from[1] = panels_ref[1, :, PW:tops]
 
     @pl.when(r > 0)
     def _():
@@ -202,11 +203,11 @@
 
     @pl.when(is_middle)
     def _():
-        pl.semaphore_wait(barrier, n_peer + 2)
+        pl.semaphore_wait(barrier, n_col + 1)
 
     @pl.when(is_first | is_last)
     def _():
-        pl.semaphore_wait(barrier, n_peer + 1)
+        pl.semaphore_wait(barrier, n_col)
 
     def l_copy(d):
         return pltpu.make_async_remote_copy(
@@ -215,7 +216,7 @@
         )
 
     def f_copy(k, d):
-        at = pl.ds(pl.multiple_of(k * kc, 8), kc)
+        at = pl.ds(k * kc, kc)
         return pltpu.make_async_remote_copy(
             src_ref=f_out.at[d, at], dst_ref=f_in.at[d, at],
             send_sem=f_sem.at[0, d, k], recv_sem=f_sem.at[1, d, k],
@@ -223,7 +224,7 @@
         )
 
     diag_copy = pltpu.make_async_remote_copy(
-        src_ref=g.at[DIAG, c], dst_ref=g.at[DIAG, c], send_sem=d_sem.at[0], recv_sem=d_sem.at[1],
+        src_ref=d_from, dst_ref=d_from, send_sem=d_sem.at[0], recv_sem=d_sem.at[1],
         device_id={"row": r + 1}, device_id_type=MESH,
     )
 
@@ -241,15 +242,18 @@
             l_copy(d).start()
 
     def f_step(k, d):
-        @pl.when(arrives(d))
-        def _():
-            f_copy(k, d).wait_recv()
-
-        @pl.when(is_middle)
-        def _():
-            at = pl.ds(pl.multiple_of(k * kc, 8), kc)
-            f_out[d, at, :] = jnp.where(from_here(q), f_out[d, at, :], f_in[d, at, :])
-            f_copy(k, d).start()
+        at = pl.ds(k * kc, kc)
+        f_copy(k, d).wait_recv()
+        f_out[d, at, :] = jnp.where(from_here(q), f_out[d, at, :], f_in[d, at, :])
+        f_copy(k, d).start()
+
+    def f_both(k):
+        if k < chunks:
+            @pl.when(is_middle)
+            def _():
+                upper = jnp.where(is_upper, 1, 0)
+                f_step(k, upper)
+                f_step(k, 1 - upper)
 
     def slot_ref(kind, slot):
         return g_top.at[slot] if kind == TOP else g.at[kind, slot]
@@ -273,6 +277,32 @@
             peer_copy(kind, m, c).start()
         sib_copy(kind, 0, c).start()
 
+    def diag_peer(m):
+        return pltpu.make_async_remote_copy(
+            src_ref=d_from.at[p], dst_ref=g_diag.at[c],
+            send_sem=peer_send.at[DIAG, m], recv_sem=peer_recv.at[DIAG, m],
+            device_id={"col": (c + 2 * m) % n_col}, device_id_type=MESH,
+        )
+
+    def diag_cross(m):
+        return pltpu.make_async_remote_copy(
+            src_ref=d_from.at[1 - p], dst_ref=g_diag.at[c],
+            send_sem=sib_send.at[DIAG, m], recv_sem=sib_recv.at[DIAG, m],
+            device_id={"col": (sibling + 2 * m) % n_col}, device_id_type=MESH,
+        )
+
+    def spread_diag():
+        for m in range(n_peer - 1, 0, -1):
+            diag_peer(m).start()
+            diag_cross(m).start()
+        diag_cross(0).start()
+        g_diag[c] = d_from[p]
+
+    inverse_copy = pltpu.make_async_remote_copy(
+        src_ref=inverse_ref.at[p], dst_ref=inverse_ref.at[p], send_sem=i_sem.at[0], recv_sem=i_sem.at[1],
+        device_id={"col": sibling}, device_id_type=MESH,
+    )
+
     def share(kind):
         for m in range(1, n_peer):
             slot = (c + n_col - 2 * m) % n_col
@@ -292,7 +322,7 @@
     @pl.when(is_first)
     def _():
         diag_copy.start()
-        spread(DIAG)
+        spread_diag()
         l_copy(0).start()
         for k in range(chunks):
             f_copy(k, 0).start()
@@ -315,7 +345,7 @@
         def _():
             diag_copy.start()
 
-        spread(DIAG)
+        spread_diag()
 
     l_step(0)
 
@@ -326,6 +356,7 @@
     top_rows = jnp.where(second < start_f, l_in[0], jnp.where(from_here(second), own_top, l_in[1]))
     g_top[c] = top_rows
     spread(TOP)
+    f_both(0)
 
     @pl.when(r > 0)
     def _():
@@ -335,90 +366,79 @@
         spread(ZERO)
         spread(ONE)
 
-    def strict(p):
-        upper = g[DIAG, :, :, p * PW : (p + 1) * PW].reshape(PW, PW)
-        return jnp.where(iota((PW, PW), 0) < iota((PW, PW), 1), upper, 0.0)
+    f_both(1)
+
+    for m in range(n_peer):
+        diag_cross(m).wait_recv()
+        if m:
+            diag_peer(m).wait_recv()
+    whole = jnp.where(iota((PW, PW), 0) < iota((PW, PW), 1), g_diag[...].reshape(PW, PW), 0.0)
+    lanes = iota((SMALL, PW), 1)
+    small = jnp.zeros((SMALL, PW), F32)
+    for b in range(PW // SMALL):
+        small += jnp.where(lanes // SMALL == b, whole[b * SMALL : (b + 1) * SMALL], 0.0)
 
     def spaced(small):
         same = iota((PW, PW), 0) // SMALL == iota((PW, PW), 1) // SMALL
-        return jnp.where(same, jnp.concatenate([small] * (PW // SMALL), 0), 0.0)
-
-    def begin():
-        share(DIAG)
-        settle(DIAG)
-        lanes = iota((SMALL, PW), 1)
-        for p in range(2):
-            whole = strict(p)
-            small = jnp.zeros((SMALL, PW), F32)
-            for b in range(PW // SMALL):
-                small += jnp.where(lanes // SMALL == b, whole[b * SMALL : (b + 1) * SMALL], 0.0)
-            small_ref[p] = one_hot(lanes % SMALL == iota((SMALL, PW), 0)) - small
-            power_ref[p] = dot_split(split(small), split(spaced(small)))
-
-    def double(_, carry):
-        for p in range(2):
-            power, small = power_ref[p], small_ref[p]
-            new = dot_split(split(jnp.concatenate([power, small], 0)), split(spaced(power)))
-            power_ref[p] = new[:SMALL]
-            small_ref[p] = small + new[SMALL:]
-        return carry
-
-    def widen():
-        for p in range(2):
-            inverse_ref[p] = spaced(small_ref[p])
-
-    def merge(level):
-        shift = SMALL.bit_length() - 1 + level
-        row, col = iota((PW, PW), 0), iota((PW, PW), 1)
-        pair = ((row >> (shift + 1)) == (col >> (shift + 1))) & ((row >> shift) != (col >> shift))
-        for p in range(2):
-            inverse = inverse_ref[p]
-            parts = split(inverse)
-            right = dot_split(split(jnp.where(pair, strict(p), 0.0)), parts)
-            inverse_ref[p] = inverse - dot_split(parts, split(right))
-
-    doublings = SMALL.bit_length() - 2
-    merges = (PW // SMALL).bit_length() - 1
-
-    def turn(k, carry):
-        @pl.when(k < chunks)
-        def _():
-            upper = jnp.where(is_upper, 1, 0)
-            f_step(k, upper)
-            f_step(k, 1 - upper)
-
-        @pl.when(k == 0)
-        def _():
-            begin()
-
-        @pl.when(k == 1)
-        def _():
-            share(TOP)
-
-        @pl.when((k == 2) & (r > 0))
-        def _():
-            share(ZERO)
-
-        @pl.when((k == 3) & (r > 0))
-        def _():
-            share(ONE)
-
-        @pl.when(k < 2)
-        def _():
-            lax.fori_loop(0, doublings // 2, double, 0)
-
-        @pl.when(k == 2)
-        def _():
-            widen()
-
-        @pl.when(k >= 2)
-        def _():
-            merge(k - 2)
-
-        return carry
-
-    lax.fori_loop(0, 2 + merges, turn, 0)
+        return split(jnp.where(same, jnp.concatenate([small] * (PW // SMALL), 0), 0.0))
+
+    power = dot_split(split(small), spaced(small))
+    small = one_hot(lanes % SMALL == iota((SMALL, PW), 0)) - small
+    span = 2
+    while span < SMALL:
+        last_one = 2 * span >= SMALL
+        new = dot_split(split(small if last_one else jnp.concatenate([small, power], 0)), spaced(power))
+        small = small + new[:SMALL]
+        power = new[SMALL:]
+        span *= 2
+        if span == 8:
+            f_both(2)
+    f_both(3)
+    for k in range(4, chunks):
+        f_both(k)
+    share(TOP)
+
+    same = iota((PW, PW), 0) // SMALL == iota((PW, PW), 1) // SMALL
+    inverse = jnp.where(same, jnp.concatenate([small] * (PW // SMALL), 0), 0.0)
+    size = SMALL
+    while size < PW:
+        pairs = PW // (2 * size)
+        pair_lanes = iota((size, PW), 1) // (2 * size)
+
+        def fold(a):
+            return sum(a[2 * size * i : 2 * size * i + size] for i in range(pairs))
+
+        def unfold(a):
+            empty = jnp.zeros((size, PW), F32)
+            return jnp.concatenate([x for i in range(pairs) for x in (jnp.where(pair_lanes == i, a, 0.0), empty)], 0)
+
+        other = (iota((size, PW), 1) // size) % 2 == 1
+        beside = sum(
+            jnp.where(other & (pair_lanes == i), whole[2 * size * i : 2 * size * i + size], 0.0) for i in range(pairs)
+        )
+        right = dot_split(split(beside), split(inverse))
+        inverse = inverse - unfold(dot_split(split(fold(inverse)), split(unfold(right))))
+        size *= 2
+    inverse_ref[p] = inverse
+    inverse_copy.start()
+
+    @pl.when(r > 0)
+    def _():
+        share(ZERO)
+        share(ONE)
+
+    @pl.when(is_first)
+    def _():
+        for k in range(chunks):
+            f_copy(k, 1).wait_recv()
+
+    @pl.when(is_last)
+    def _():
+        for k in range(chunks):
+            f_copy(k, 0).wait_recv()
+
     settle(TOP)
+    inverse_copy.wait_recv()
 
     top = jnp.where(q < start_f, f_in[0], jnp.where(from_here(q), own_ref[...], f_in[1]))
     upper0_full = dot_split(split(top[:, :PW]), split(inverse_ref[0]))
@@ -443,7 +463,11 @@
         drain(ZERO)
         drain(ONE)
 
-    drain(DIAG)
+    for m in range(n_peer):
+        diag_cross(m).wait_send()
+        if m:
+            diag_peer(m).wait_send()
+    inverse_copy.wait_send()
     drain(TOP)
 
     @pl.when(r < last)
@@ -472,16 +496,17 @@
         in_specs=[vmem] * 3,
         out_specs=vmem,
         scratch_shapes=[
-            pltpu.VMEM((3, n_col, kc, rows), F32),
+            pltpu.VMEM((2, kc, PW), F32),
+            pltpu.VMEM((n_col, kc, PW), F32),
+            pltpu.VMEM((2, n_col, kc, rows), F32),
             pltpu.VMEM((n_col, kc, PW), F32),
             pltpu.VMEM((cols, tops), F32),
             pltpu.VMEM((2, cols, tops), F32),
             pltpu.VMEM((2, cols, tops), F32),
             pltpu.VMEM((2, kc, PW), F32),
             pltpu.VMEM((2, kc, PW), F32),
-            pltpu.VMEM((2, SMALL, PW), F32),
-            pltpu.VMEM((2, SMALL, PW), F32),
             pltpu.VMEM((2, PW, PW), F32),
+            dma((2,)),
             dma((2,)),
             dma((2, 2)),
             dma((2, 2, cols // kc)),
@@ -499,7 +524,6 @@
         block.shape[0] == 2 * PW
         and block.shape[1] % 128 == 0
         and kc % 8 == 0
-        and block.shape[1] // kc in range(1, 6)
         and block.shape[1] % kc == 0
         and lax.axis_size("col") % 2 == 0
         and lax.axis_size("row") > 1

time: 39 us -> 34.9 us (0.89)
  Pallas kernels: 35.5 us -> 31.5 us
    pallas_call x1, Pallas kernels: 35.5 us -> 31.5 us  [fused(): pl.pallas_call(functools.partial(kernel, n_row, n_col), out_shape=jax.Sha...]
where the time goes in v4:
time: 34.9 us; the launch traced here: 34.7 us
  Pallas kernels  31.5 us (90%)
  local copies, waits for them, and re-layouts  3.24 us (9%)
    pallas_call x1, Pallas kernels, fused(): pl.pallas_call(functools.partial(kernel, n_row, n_col), out_shape=jax.Sha...  31.5 us
    unnamed x7, local copies, waits for them, and re-layouts  3.24 us

profile of v4, /device:TPU:0, one launch (start us, length us, event | category | flops | bytes accessed | tf_op | source)
XLA Modules:
  0.0 34.7 jit_solution(7781553132531372947)
XLA Ops:
  0.0 0.0 copy-start
  0.0 0.9 %copy-done = f32[512,128]{1,0:T(8,128)S(1)} copy-done((f32[512,128]{1,0:T(8,128)S(1)}, f32[512,128]{1,0:T(8,128)}, u32[]{:S(2)}) %copy-start) | copy-done | bytes 262168
  1.0 0.0 copy-start.1
  1.0 0.9 %copy-done.1 = f32[2,512,32]{1,2,0:T(8,128)S(1)} copy-done((f32[2,512,32]{1,2,0:T(8,128)S(1)}, f32[2,512,32]{1,2,0:T(8,128)}, u32[]{:S(2)}) %copy-start.1) | copy-done | bytes 131096
  1.9 0.0 copy-start.2
  1.9 0.7 %copy-done.2 = s32[2,256]{1,0:T(2,128)S(1)} copy-done((s32[2,256]{1,0:T(2,128)S(1)}, s32[2,256]{1,0:T(2,128)}, u32[]{:S(2)}) %copy-start.2) | copy-done | bytes 2072
  2.5 31.5 %shard_map.37 = f32[512,128]{1,0:T(8,128)S(1)} custom-call(s32[2,256]{1,0:T(2,128)S(1)} %copy-done.2, f32[512,128]{1,0:T(8,128)S(1)} %copy-done, f32[2,32,512]{2,1,0:T(8,128)S(1)} %bitcast.1), custom_call_target="tpu_custom_call" | custom-call | tf_op jit(solution)/shard_map/pallas_call | solution.py:493
  34.0 0.7 %copy.5 = f32[512,128]{1,0:T(8,128)} copy(f32[512,128]{1,0:T(8,128)S(1)} %shard_map.37) | data formatting | bytes 524288
Async XLA Ops:
  0.0 0.9 %copy-start = (f32[512,128]{1,0:T(8,128)S(1)}, f32[512,128]{1,0:T(8,128)}, u32[]{:S(2)}) copy-start(f32[512,128]{1,0:T(8,128)} %block_ref.1) | copy-start | bytes 786436
  1.0 0.9 %copy-start.1 = (f32[2,512,32]{1,2,0:T(8,128)S(1)}, f32[2,512,32]{1,2,0:T(8,128)}, u32[]{:S(2)}) copy-start(f32[2,512,32]{1,2,0:T(8,128)} %param.4) | copy-start | bytes 393220
  1.9 0.7 %copy-start.2 = (s32[2,256]{1,0:T(2,128)S(1)}, s32[2,256]{1,0:T(2,128)}, u32[]{:S(2)}) copy-start(s32[2,256]{1,0:T(2,128)} %piv_ref.1) | copy-start | bytes 6148

commit v5 on v4

--- a/solution.py
+++ b/solution.py
@@ -83,6 +83,7 @@
 MESH = pl.DeviceIdType.MESH
 F32, BF16 = jnp.float32, jnp.bfloat16
 SMALL = 32
+PART = 16
 ONE, ZERO, TOP, DIAG = range(4)
 
 
@@ -103,12 +104,8 @@
 
 def dot_pick(a, one_hot):
     m = a.shape[0]
-    high = a.astype(BF16)
-    rest = a - high.astype(F32)
-    mid = rest.astype(BF16)
-    low = (rest - mid.astype(F32)).astype(BF16)
-    out = dot(jnp.concatenate([high, mid, low], 0), one_hot)
-    return out[:m] + (out[m : 2 * m] + out[2 * m :])
+    out = dot(jnp.concatenate(split(a), 0), one_hot)
+    return out[:m] + out[m:]
 
 
 def iota(shape, dim):
@@ -122,6 +119,7 @@
 def kernel(
     n_row, n_col, piv_ref, block_ref, panels_ref, out_ref, d_from, g_diag,
     g, g_top, own_ref, f_in, f_out, l_in, l_out, inverse_ref,
+    block_t, put_ref, moved_ref, low_high, low_low,
     d_sem, i_sem, l_sem, f_sem, peer_send, peer_recv, sib_send, sib_recv,
 ):
     r, c = lax.axis_index("row"), lax.axis_index("col")
@@ -129,7 +127,7 @@
     tops = 2 * PW
     kc = panels_ref.shape[1]
     n_peer = n_col // 2
-    chunks = cols // kc
+    chunks = cols // PART
     last = n_row - 1
     p = c % 2
     sibling = c + 1 - 2 * p
@@ -183,15 +181,6 @@
     def from_here(v):
         return (v >= start_f) & (v < start_f + rows)
 
-    own_top = dot_pick(panels_ref[0], one_hot(iota((rows, PW), 0).astype(F32) == local_one).astype(BF16))
-    l_out[0] = own_top
-    l_out[1] = own_top
-    block_t = block_ref[...].T
-    own = dot_pick(block_t, one_hot(iota((rows, tops), 0).astype(F32) == local).astype(BF16))
-    own_ref[...] = own
-    f_out[0] = own
-    f_out[1] = own
-
     @pl.when(is_first)
     def _():
         d_from[0] = panels_ref[0, :, :PW]
@@ -216,7 +205,7 @@
         )
 
     def f_copy(k, d):
-        at = pl.ds(k * kc, kc)
+        at = pl.ds(k * PART, PART)
         return pltpu.make_async_remote_copy(
             src_ref=f_out.at[d, at], dst_ref=f_in.at[d, at],
             send_sem=f_sem.at[0, d, k], recv_sem=f_sem.at[1, d, k],
@@ -242,7 +231,7 @@
             l_copy(d).start()
 
     def f_step(k, d):
-        at = pl.ds(k * kc, kc)
+        at = pl.ds(k * PART, PART)
         f_copy(k, d).wait_recv()
         f_out[d, at, :] = jnp.where(from_here(q), f_out[d, at, :], f_in[d, at, :])
         f_copy(k, d).start()
@@ -323,6 +312,22 @@
     def _():
         diag_copy.start()
         spread_diag()
+
+    @pl.when(r > 0)
+    def _():
+        spread(ONE)
+
+    own_top = dot_pick(panels_ref[0], one_hot(iota((rows, PW), 0).astype(F32) == local_one).astype(BF16))
+    l_out[0] = own_top
+    l_out[1] = own_top
+    block_t[...] = block_ref[...].T
+    own = dot_pick(block_t[...], one_hot(iota((rows, tops), 0).astype(F32) == local).astype(BF16))
+    own_ref[...] = own
+    f_out[0] = own
+    f_out[1] = own
+
+    @pl.when(is_first)
+    def _():
         l_copy(0).start()
         for k in range(chunks):
             f_copy(k, 0).start()
@@ -364,9 +369,9 @@
         moved = jnp.sum(put, axis=0, keepdims=True) > 0.5
         g[ZERO, c] = jnp.where(moved, dot_pick(l_in[0], put.astype(BF16)), panels_ref[0])
         spread(ZERO)
-        spread(ONE)
 
     f_both(1)
+    f_both(2)
 
     for m in range(n_peer):
         diag_cross(m).wait_recv()
@@ -383,6 +388,7 @@
         return split(jnp.where(same, jnp.concatenate([small] * (PW // SMALL), 0), 0.0))
 
     power = dot_split(split(small), spaced(small))
+    f_both(3)
     small = one_hot(lanes % SMALL == iota((SMALL, PW), 0)) - small
     span = 2
     while span < SMALL:
@@ -391,11 +397,7 @@
         small = small + new[:SMALL]
         power = new[SMALL:]
         span *= 2
-        if span == 8:
-            f_both(2)
-    f_both(3)
-    for k in range(4, chunks):
-        f_both(k)
+        f_both(span.bit_length() + 1)
     share(TOP)
 
     same = iota((PW, PW), 0) // SMALL == iota((PW, PW), 1) // SMALL
@@ -419,6 +421,8 @@
         right = dot_split(split(beside), split(inverse))
         inverse = inverse - unfold(dot_split(split(fold(inverse)), split(unfold(right))))
         size *= 2
+    for k in range(8, chunks):
+        f_both(k)
     inverse_ref[p] = inverse
     inverse_copy.start()
 
@@ -427,39 +431,52 @@
         share(ZERO)
         share(ONE)
 
-    @pl.when(is_first)
-    def _():
-        for k in range(chunks):
-            f_copy(k, 1).wait_recv()
-
-    @pl.when(is_last)
-    def _():
-        for k in range(chunks):
-            f_copy(k, 0).wait_recv()
+    @pl.when(r > 0)
+    def _():
+        put = one_hot(iota((tops, rows), 1).astype(F32) == q_c - start_f)
+        moved_ref[0:1, :] = jnp.sum(put, axis=0, keepdims=True)
+        put_ref[...] = put.astype(BF16)
+        for kind, at in ((ZERO, 0), (ONE, PW)):
+            settle(kind)
+            high, low = split(g[kind].reshape(PW, rows))
+            low_high[at : at + PW] = high
+            low_low[at : at + PW] = low
 
     settle(TOP)
+    above = split(g_top[...].reshape(PW, PW))
     inverse_copy.wait_recv()
-
-    top = jnp.where(q < start_f, f_in[0], jnp.where(from_here(q), own_ref[...], f_in[1]))
-    upper0_full = dot_split(split(top[:, :PW]), split(inverse_ref[0]))
-    upper0 = split(upper0_full)
-    rest = top[:, PW:] - dot_split(upper0, split(g_top[...].reshape(PW, PW)))
-    upper1_full = dot_split(split(rest), split(inverse_ref[1]))
-
-    @pl.when(is_first)
-    def _():
-        out_ref[...] = jnp.concatenate([upper0_full, upper1_full], 1).T
-
-    @pl.when(r > 0)
-    def _():
-        settle(ZERO)
-        settle(ONE)
-        put = one_hot(iota((tops, rows), 1).astype(F32) == q_c - start_f)
-        moved = jnp.sum(put, axis=0, keepdims=True) > 0.5
-        work = jnp.where(moved, dot_pick(f_in[0], put.astype(BF16)), block_ref[...].T)
-        work = work - dot_split(upper0, split(g[ZERO].reshape(PW, rows)))
-        work = work - dot_split(split(upper1_full), split(g[ONE].reshape(PW, rows)))
-        out_ref[...] = work.T
+    inverses = [split(inverse_ref[0]), split(inverse_ref[1])]
+
+    for half in range(2):
+        mine = range(half * chunks // 2, (half + 1) * chunks // 2)
+        at = slice(mine[0] * PART, (mine[-1] + 1) * PART)
+
+        @pl.when(is_first)
+        def _():
+            for k in mine:
+                f_copy(k, 1).wait_recv()
+
+        @pl.when(is_last)
+        def _():
+            for k in mine:
+                f_copy(k, 0).wait_recv()
+
+        top = jnp.where(q < start_f, f_in[0, at], jnp.where(from_here(q), own_ref[at], f_in[1, at]))
+        upper0 = dot_split(split(top[:, :PW]), inverses[0])
+        upper1 = dot_split(split(top[:, PW:] - dot_split(split(upper0), above)), inverses[1])
+        upper = jnp.concatenate([upper0, upper1], 1)
+
+        @pl.when(is_first)
+        def _():
+            out_ref[:, at] = upper.T
+
+        @pl.when(r > 0)
+        def _():
+            work = jnp.where(moved_ref[0:1, :] > 0.5, dot_pick(f_in[0, at], put_ref[...]), block_t[at])
+            out_ref[:, at] = (work - dot_split(split(upper), (low_high[...], low_low[...]))).T
+
+    @pl.when(r > 0)
+    def _():
         drain(ZERO)
         drain(ONE)
 
@@ -506,10 +523,15 @@
             pltpu.VMEM((2, kc, PW), F32),
             pltpu.VMEM((2, kc, PW), F32),
             pltpu.VMEM((2, PW, PW), F32),
+            pltpu.VMEM((cols, rows), F32),
+            pltpu.VMEM((tops, rows), BF16),
+            pltpu.VMEM((8, rows), F32),
+            pltpu.VMEM((tops, rows), BF16),
+            pltpu.VMEM((tops, rows), BF16),
             dma((2,)),
             dma((2,)),
             dma((2, 2)),
-            dma((2, 2, cols // kc)),
+            dma((2, 2, cols // PART)),
         ]
         + [dma((4, n_peer))] * 4,
         compiler_params=pltpu.CompilerParams(
@@ -524,7 +546,6 @@
         block.shape[0] == 2 * PW
         and block.shape[1] % 128 == 0
         and kc % 8 == 0
-        and block.shape[1] % kc == 0
         and lax.axis_size("col") % 2 == 0
         and lax.axis_size("row") > 1
     )

time: 34.9 us -> 45.5 us (1.30)
  Pallas kernels: 31.5 us -> 41.8 us
    pallas_call x1, Pallas kernels: 31.5 us -> 41.8 us  [fused(): pl.pallas_call(functools.partial(kernel, n_row, n_col), out_shape=jax.Sha...]
where the time goes in v5:
time: 45.5 us; the launch traced here: 45.1 us
  Pallas kernels  41.8 us (92%)
  local copies, waits for them, and re-layouts  3.24 us (7%)
    pallas_call x1, Pallas kernels, fused(): pl.pallas_call(functools.partial(kernel, n_row, n_col), out_shape=jax.Sha...  41.8 us
    unnamed x7, local copies, waits for them, and re-layouts  3.24 us

profile of v5, /device:TPU:0, one launch (start us, length us, event | category | flops | bytes accessed | tf_op | source)
XLA Modules:
  0.0 45.1 jit_solution(4678781504805671416)
XLA Ops:
  0.0 0.0 copy-start
  0.0 0.9 %copy-done = f32[512,128]{1,0:T(8,128)S(1)} copy-done((f32[512,128]{1,0:T(8,128)S(1)}, f32[512,128]{1,0:T(8,128)}, u32[]{:S(2)}) %copy-start) | copy-done | bytes 262168
  1.0 0.0 copy-start.1
  1.0 0.9 %copy-done.1 = f32[2,512,32]{1,2,0:T(8,128)S(1)} copy-done((f32[2,512,32]{1,2,0:T(8,128)S(1)}, f32[2,512,32]{1,2,0:T(8,128)}, u32[]{:S(2)}) %copy-start.1) | copy-done | bytes 131096
  1.9 0.0 copy-start.2
  1.9 0.7 %copy-done.2 = s32[2,256]{1,0:T(2,128)S(1)} copy-done((s32[2,256]{1,0:T(2,128)S(1)}, s32[2,256]{1,0:T(2,128)}, u32[]{:S(2)}) %copy-start.2) | copy-done | bytes 2072
  2.5 41.8 %shard_map.37 = f32[512,128]{1,0:T(8,128)S(1)} custom-call(s32[2,256]{1,0:T(2,128)S(1)} %copy-done.2, f32[512,128]{1,0:T(8,128)S(1)} %copy-done, f32[2,32,512]{2,1,0:T(8,128)S(1)} %bitcast.1), custom_call_target="tpu_custom_call" | custom-call | tf_op jit(solution)/shard_map/pallas_call | solution.py:510
  44.4 0.7 %copy.5 = f32[512,128]{1,0:T(8,128)} copy(f32[512,128]{1,0:T(8,128)S(1)} %shard_map.37) | data formatting | bytes 524288
Async XLA Ops:
  0.0 0.9 %copy-start = (f32[512,128]{1,0:T(8,128)S(1)}, f32[512,128]{1,0:T(8,128)}, u32[]{:S(2)}) copy-start(f32[512,128]{1,0:T(8,128)} %block_ref.1) | copy-start | bytes 786436
  1.0 0.9 %copy-start.1 = (f32[2,512,32]{1,2,0:T(8,128)S(1)}, f32[2,512,32]{1,2,0:T(8,128)}, u32[]{:S(2)}) copy-start(f32[2,512,32]{1,2,0:T(8,128)} %param.4) | copy-start | bytes 393220
  1.9 0.7 %copy-start.2 = (s32[2,256]{1,0:T(2,128)S(1)}, s32[2,256]{1,0:T(2,128)}, u32[]{:S(2)}) copy-start(s32[2,256]{1,0:T(2,128)} %piv_ref.1) | copy-start | bytes 6148

commit v6 on v5

--- a/solution.py
+++ b/solution.py
@@ -83,7 +83,8 @@
 MESH = pl.DeviceIdType.MESH
 F32, BF16 = jnp.float32, jnp.bfloat16
 SMALL = 32
-PART = 16
+PART = 32
+LAG = 2
 ONE, ZERO, TOP, DIAG = range(4)
 
 
@@ -236,13 +237,16 @@
         f_out[d, at, :] = jnp.where(from_here(q), f_out[d, at, :], f_in[d, at, :])
         f_copy(k, d).start()
 
-    def f_both(k):
-        if k < chunks:
+    def stage(k):
+        upper = jnp.where(is_upper, 1, 0)
+        near, far = k < chunks, 0 <= k - LAG < chunks
+        if near or far:
             @pl.when(is_middle)
             def _():
-                upper = jnp.where(is_upper, 1, 0)
-                f_step(k, upper)
-                f_step(k, 1 - upper)
+                if near:
+                    f_step(k, upper)
+                if far:
+                    f_step(k - LAG, 1 - upper)
 
     def slot_ref(kind, slot):
         return g_top.at[slot] if kind == TOP else g.at[kind, slot]
@@ -361,7 +365,7 @@
     top_rows = jnp.where(second < start_f, l_in[0], jnp.where(from_here(second), own_top, l_in[1]))
     g_top[c] = top_rows
     spread(TOP)
-    f_both(0)
+    stage(0)
 
     @pl.when(r > 0)
     def _():
@@ -370,8 +374,8 @@
         g[ZERO, c] = jnp.where(moved, dot_pick(l_in[0], put.astype(BF16)), panels_ref[0])
         spread(ZERO)
 
-    f_both(1)
-    f_both(2)
+    stage(1)
+    stage(2)
 
     for m in range(n_peer):
         diag_cross(m).wait_recv()
@@ -388,7 +392,7 @@
         return split(jnp.where(same, jnp.concatenate([small] * (PW // SMALL), 0), 0.0))
 
     power = dot_split(split(small), spaced(small))
-    f_both(3)
+    stage(3)
     small = one_hot(lanes % SMALL == iota((SMALL, PW), 0)) - small
     span = 2
     while span < SMALL:
@@ -397,7 +401,7 @@
         small = small + new[:SMALL]
         power = new[SMALL:]
         span *= 2
-        f_both(span.bit_length() + 1)
+        stage(span.bit_length() + 1)
     share(TOP)
 
     same = iota((PW, PW), 0) // SMALL == iota((PW, PW), 1) // SMALL
@@ -421,8 +425,8 @@
         right = dot_split(split(beside), split(inverse))
         inverse = inverse - unfold(dot_split(split(fold(inverse)), split(unfold(right))))
         size *= 2
-    for k in range(8, chunks):
-        f_both(k)
+    for k in range(8, chunks + LAG):
+        stage(k)
     inverse_ref[p] = inverse
     inverse_copy.start()
 

time: 45.5 us -> 27.9 us (0.61)
  Pallas kernels: 41.8 us -> 24.2 us
    pallas_call x1, Pallas kernels: 41.8 us -> 24.2 us  [fused(): pl.pallas_call(functools.partial(kernel, n_row, n_col), out_shape=jax.Sha...]
where the time goes in v6:
time: 27.9 us; the launch traced here: 27.5 us
  Pallas kernels  24.2 us (87%)
  local copies, waits for them, and re-layouts  3.24 us (12%)
    pallas_call x1, Pallas kernels, fused(): pl.pallas_call(functools.partial(kernel, n_row, n_col), out_shape=jax.Sha...  24.2 us
    unnamed x7, local copies, waits for them, and re-layouts  3.24 us

profile of v6, /device:TPU:0, one launch (start us, length us, event | category | flops | bytes accessed | tf_op | source)
XLA Modules:
  0.0 27.5 jit_solution(11186524250386680531)
XLA Ops:
  0.0 0.0 copy-start
  0.0 0.9 %copy-done = f32[512,128]{1,0:T(8,128)S(1)} copy-done((f32[512,128]{1,0:T(8,128)S(1)}, f32[512,128]{1,0:T(8,128)}, u32[]{:S(2)}) %copy-start) | copy-done | bytes 262168
  1.0 0.0 copy-start.1
  1.0 0.9 %copy-done.1 = f32[2,512,32]{1,2,0:T(8,128)S(1)} copy-done((f32[2,512,32]{1,2,0:T(8,128)S(1)}, f32[2,512,32]{1,2,0:T(8,128)}, u32[]{:S(2)}) %copy-start.1) | copy-done | bytes 131096
  1.9 0.0 copy-start.2
  1.9 0.7 %copy-done.2 = s32[2,256]{1,0:T(2,128)S(1)} copy-done((s32[2,256]{1,0:T(2,128)S(1)}, s32[2,256]{1,0:T(2,128)}, u32[]{:S(2)}) %copy-start.2) | copy-done | bytes 2072
  2.5 24.2 %shard_map.37 = f32[512,128]{1,0:T(8,128)S(1)} custom-call(s32[2,256]{1,0:T(2,128)S(1)} %copy-done.2, f32[512,128]{1,0:T(8,128)S(1)} %copy-done, f32[2,32,512]{2,1,0:T(8,128)S(1)} %bitcast.1), custom_call_target="tpu_custom_call" | custom-call | tf_op jit(solution)/shard_map/pallas_call | solution.py:514
  26.8 0.7 %copy.5 = f32[512,128]{1,0:T(8,128)} copy(f32[512,128]{1,0:T(8,128)S(1)} %shard_map.37) | data formatting | bytes 524288
Async XLA Ops:
  0.0 0.9 %copy-start = (f32[512,128]{1,0:T(8,128)S(1)}, f32[512,128]{1,0:T(8,128)}, u32[]{:S(2)}) copy-start(f32[512,128]{1,0:T(8,128)} %block_ref.1) | copy-start | bytes 786436
  1.0 0.9 %copy-start.1 = (f32[2,512,32]{1,2,0:T(8,128)S(1)}, f32[2,512,32]{1,2,0:T(8,128)}, u32[]{:S(2)}) copy-start(f32[2,512,32]{1,2,0:T(8,128)} %param.4) | copy-start | bytes 393220
  1.9 0.7 %copy-start.2 = (s32[2,256]{1,0:T(2,128)S(1)}, s32[2,256]{1,0:T(2,128)}, u32[]{:S(2)}) copy-start(s32[2,256]{1,0:T(2,128)} %piv_ref.1) | copy-start | bytes 6148

commit v7 on v6

--- a/solution.py
+++ b/solution.py
@@ -118,15 +118,15 @@
 
 
 def kernel(
-    n_row, n_col, piv_ref, block_ref, panels_ref, out_ref, d_from, g_diag,
+    n_row, n_col, block_ref, panels_ref, out_ref, d_from, g_diag,
     g, g_top, own_ref, f_in, f_out, l_in, l_out, inverse_ref,
-    block_t, put_ref, moved_ref, low_high, low_low,
+    block_t, local_ref, put_ref, put_one_ref, moved_ref, low_high, low_low,
     d_sem, i_sem, l_sem, f_sem, peer_send, peer_recv, sib_send, sib_recv,
 ):
     r, c = lax.axis_index("row"), lax.axis_index("col")
     rows, cols = block_ref.shape
     tops = 2 * PW
-    kc = panels_ref.shape[1]
+    kc = g_top.shape[1]
     n_peer = n_col // 2
     chunks = cols // PART
     last = n_row - 1
@@ -150,14 +150,14 @@
     for m in range(1, n_col):
         pl.semaphore_signal(barrier, 1, device_id={"col": (c + m) % n_col}, device_id_type=MESH)
 
-    first = piv_ref[0:1, :].astype(F32)
-    second = piv_ref[1:2, :].astype(F32)
+    first = panels_ref[2 * kc : 2 * kc + 1, :PW]
+    second = panels_ref[2 * kc + 1 : 2 * kc + 2, :PW]
     sub, lane = iota((PW, PW), 0).astype(F32), iota((PW, PW), 1).astype(F32)
 
     def upright(v):
         return jnp.sum(jnp.where(sub == lane, v, 0.0), axis=1, keepdims=True)
 
-    first_c, second_c = upright(first), upright(second)
+    first_c = upright(first)
     lane_row = lane[0:1, :]
     sub_col = sub[:, 0:1]
 
@@ -166,30 +166,32 @@
         return jnp.sum(jnp.where(match, found, 0.0), axis=axis, keepdims=True) + jnp.where(hit > 0.5, 0.0, otherwise)
 
     q_second = lookup(first_c == second, sub, second, 0)
-    q_second_c = lookup(second_c == first, lane, second_c, 1)
-    home = lookup(first_c == lane + PW, sub, lane_row + PW, 0)
-    home_c = lookup(first == sub + PW, lane, sub_col + PW, 1)
-    out_first = jnp.where(first < tops, first, lookup(second_c == first, home_c, lane_row, 0))
-    out_second = jnp.where(q_second < tops, q_second, home)
     q = jnp.concatenate([first, q_second], 1)
-    q_c = jnp.concatenate([first_c, q_second_c], 0)
-    outward = jnp.concatenate([out_first, out_second], 1)
-
     start_f = start.astype(F32)
-    local = jnp.where(is_first, outward, q - start_f)
-    local_one = jnp.where(is_first, lane_row + PW, second - start_f)
+    local_ref[0:1, :] = q - start_f
+    local_ref[1:2, :PW] = second - start_f
+
+    @pl.when(is_first)
+    def _():
+        second_c = upright(second)
+        home = lookup(first_c == lane + PW, sub, lane_row + PW, 0)
+        home_c = lookup(first == sub + PW, lane, sub_col + PW, 1)
+        out_first = jnp.where(first < tops, first, lookup(second_c == first, home_c, lane_row, 0))
+        out_second = jnp.where(q_second < tops, q_second, home)
+        local_ref[0:1, :] = jnp.concatenate([out_first, out_second], 1)
+        local_ref[1:2, :PW] = lane_row + PW
 
     def from_here(v):
         return (v >= start_f) & (v < start_f + rows)
 
     @pl.when(is_first)
     def _():
-        d_from[0] = panels_ref[0, :, :PW]
-        d_from[1] = panels_ref[1, :, PW:tops]
-
-    @pl.when(r > 0)
-    def _():
-        g[ONE, c] = panels_ref[1]
+        d_from[0] = panels_ref[:kc, :PW]
+        d_from[1] = panels_ref[kc : 2 * kc, PW:tops]
+
+    @pl.when(r > 0)
+    def _():
+        g[ONE, c] = panels_ref[kc : 2 * kc]
 
     @pl.when(is_middle)
     def _():
@@ -321,26 +323,44 @@
     def _():
         spread(ONE)
 
-    own_top = dot_pick(panels_ref[0], one_hot(iota((rows, PW), 0).astype(F32) == local_one).astype(BF16))
+    own_top = dot_pick(panels_ref[:kc], one_hot(iota((rows, PW), 0).astype(F32) == local_ref[1:2, :PW]).astype(BF16))
     l_out[0] = own_top
     l_out[1] = own_top
+
+    @pl.when(is_first)
+    def _():
+        l_copy(0).start()
+
+    @pl.when(is_last)
+    def _():
+        l_copy(1).start()
+
     block_t[...] = block_ref[...].T
-    own = dot_pick(block_t[...], one_hot(iota((rows, tops), 0).astype(F32) == local).astype(BF16))
+    own = dot_pick(block_t[...], one_hot(iota((rows, tops), 0).astype(F32) == local_ref[0:1, :]).astype(BF16))
     own_ref[...] = own
     f_out[0] = own
     f_out[1] = own
 
     @pl.when(is_first)
     def _():
-        l_copy(0).start()
         for k in range(chunks):
             f_copy(k, 0).start()
 
     @pl.when(is_last)
     def _():
-        l_copy(1).start()
         for k in range(chunks):
             f_copy(k, 1).start()
+
+    @pl.when(r > 0)
+    def _():
+        second_c = upright(second)
+        q_c = jnp.concatenate([first_c, lookup(second_c == first, lane, second_c, 1)], 0)
+        put = one_hot(iota((PW, rows), 1).astype(F32) == second_c - start_f)
+        put_one_ref[...] = put.astype(BF16)
+        moved_ref[1:2, :] = jnp.sum(put, axis=0, keepdims=True)
+        put = one_hot(iota((tops, rows), 1).astype(F32) == q_c - start_f)
+        put_ref[...] = put.astype(BF16)
+        moved_ref[0:1, :] = jnp.sum(put, axis=0, keepdims=True)
 
     @pl.when(is_upper)
     def _():
@@ -369,9 +389,7 @@
 
     @pl.when(r > 0)
     def _():
-        put = one_hot(iota((PW, rows), 1).astype(F32) == second_c - start_f)
-        moved = jnp.sum(put, axis=0, keepdims=True) > 0.5
-        g[ZERO, c] = jnp.where(moved, dot_pick(l_in[0], put.astype(BF16)), panels_ref[0])
+        g[ZERO, c] = jnp.where(moved_ref[1:2, :] > 0.5, dot_pick(l_in[0], put_one_ref[...]), panels_ref[:kc])
         spread(ZERO)
 
     stage(1)
@@ -430,16 +448,20 @@
     inverse_ref[p] = inverse
     inverse_copy.start()
 
+    def settle_rows(at):
+        block_t[at] = jnp.where(moved_ref[0:1, :] > 0.5, dot_pick(f_in[0, at], put_ref[...]), block_t[at])
+
     @pl.when(r > 0)
     def _():
         share(ZERO)
         share(ONE)
 
-    @pl.when(r > 0)
-    def _():
-        put = one_hot(iota((tops, rows), 1).astype(F32) == q_c - start_f)
-        moved_ref[0:1, :] = jnp.sum(put, axis=0, keepdims=True)
-        put_ref[...] = put.astype(BF16)
+    @pl.when(is_middle)
+    def _():
+        settle_rows(slice(0, cols))
+
+    @pl.when(r > 0)
+    def _():
         for kind, at in ((ZERO, 0), (ONE, PW)):
             settle(kind)
             high, low = split(g[kind].reshape(PW, rows))
@@ -464,6 +486,7 @@
         def _():
             for k in mine:
                 f_copy(k, 0).wait_recv()
+            settle_rows(at)
 
         top = jnp.where(q < start_f, f_in[0, at], jnp.where(from_here(q), own_ref[at], f_in[1, at]))
         upper0 = dot_split(split(top[:, :PW]), inverses[0])
@@ -476,8 +499,7 @@
 
         @pl.when(r > 0)
         def _():
-            work = jnp.where(moved_ref[0:1, :] > 0.5, dot_pick(f_in[0, at], put_ref[...]), block_t[at])
-            out_ref[:, at] = (work - dot_split(split(upper), (low_high[...], low_low[...]))).T
+            out_ref[:, at] = (block_t[at] - dot_split(split(upper), (low_high[...], low_low[...]))).T
 
     @pl.when(r > 0)
     def _():
@@ -511,10 +533,12 @@
     vmem = pl.BlockSpec(memory_space=pltpu.VMEM)
     n_peer = n_col // 2
     dma = pltpu.SemaphoreType.DMA
+    lists = jnp.pad(pivots.astype(F32), ((0, 6), (0, rows - PW)))
+    packed = jnp.concatenate([jnp.swapaxes(panels, 1, 2).reshape(2 * kc, rows), lists], 0)
     return pl.pallas_call(
         functools.partial(kernel, n_row, n_col),
         out_shape=jax.ShapeDtypeStruct((rows, cols), F32),
-        in_specs=[vmem] * 3,
+        in_specs=[vmem] * 2,
         out_specs=vmem,
         scratch_shapes=[
             pltpu.VMEM((2, kc, PW), F32),
@@ -528,7 +552,9 @@
             pltpu.VMEM((2, kc, PW), F32),
             pltpu.VMEM((2, PW, PW), F32),
             pltpu.VMEM((cols, rows), F32),
+            pltpu.VMEM((8, rows), F32),
             pltpu.VMEM((tops, rows), BF16),
+            pltpu.VMEM((PW, rows), BF16),
             pltpu.VMEM((8, rows), F32),
             pltpu.VMEM((tops, rows), BF16),
             pltpu.VMEM((tops, rows), BF16),
@@ -541,7 +567,7 @@
         compiler_params=pltpu.CompilerParams(
             collective_id=0, has_side_effects=True, vmem_limit_bytes=48 * 1024 * 1024
         ),
-    )(pivots, block, jnp.swapaxes(panels, 1, 2))
+    )(block, packed)
 
 
 def body(block, panels, pivots):

time: 27.9 us -> 26.8 us (0.961)
  local copies, waits for them, and re-layouts: 3.24 us -> 0.71 us
  other arithmetic: 0 us -> 1.64 us
    unnamed x7 -> x3, local copies, waits for them, and re-layouts: 3.24 us -> 0.71 us
    concatenate x0 -> x1, other arithmetic: none -> 0.91 us  [fused(): jnp.concatenate([jnp.swapaxes(panels, 1, 2).reshape(2 * kc, rows), lists]...]
    convert_element_type x0 -> x1, other arithmetic: none -> 0.73 us  [fused(): lists = jnp.pad(pivots.astype(F32), ((0, 6), (0, rows - PW)))]
where the time goes in v7:
time: 26.8 us; the launch traced here: 26.5 us
  Pallas kernels  24.1 us (90%)
  other arithmetic  1.64 us (6%)
  local copies, waits for them, and re-layouts  0.71 us (3%)
    pallas_call x1, Pallas kernels, fused(): pl.pallas_call(functools.partial(kernel, n_row, n_col), out_shape=jax.Sha...  24.1 us
    concatenate x1, other arithmetic, fused(): jnp.concatenate([jnp.swapaxes(panels, 1, 2).reshape(2 * kc, rows), lists]...  0.91 us
    convert_element_type x1, other arithmetic, fused(): lists = jnp.pad(pivots.astype(F32), ((0, 6), (0, rows - PW)))  0.73 us
    unnamed x3, local copies, waits for them, and re-layouts  0.71 us

profile of v7, /device:TPU:0, one launch (start us, length us, event | category | flops | bytes accessed | tf_op | source)
XLA Modules:
  0.0 26.5 jit_solution(8752723855608682968)
XLA Ops:
  0.0 0.0 copy-start
  0.0 0.7 %convert_element_type.5 = f32[2,256]{1,0:T(2,128)S(1)} convert(s32[2,256]{1,0:T(2,128)} %param.5) | non-fusion elementwise | flops 512 | bytes 4096 | tf_op jit(solution)/shard_map/convert_element_type | solution.py:536
  0.7 0.9 %select_maximum_fusion.panels_ref = f32[72,512]{1,0:T(8,128)S(1)} fusion(f32[2,256]{1,0:T(2,128)S(1)} %convert_element_type.5, f32[64,512]{1,0:T(8,128)} %bitcast.3), kind=kLoop, calls=%fused_computation | loop fusion | flops 110592 | bytes 280576 | tf_op jit(solution)/shard_map/concatenate | solution.py:537
  1.6 0.0 copy-done
  1.7 24.1 %shard_map.37 = f32[512,128]{1,0:T(8,128)S(1)} custom-call(f32[512,128]{1,0:T(8,128)S(1)} %copy-done, f32[72,512]{1,0:T(8,128)S(1)} %select_maximum_fusion.panels_ref), custom_call_target="tpu_custom_call" | custom-call | tf_op jit(solution)/shard_map/pallas_call | solution.py:538
  25.8 0.7 %copy.5 = f32[512,128]{1,0:T(8,128)} copy(f32[512,128]{1,0:T(8,128)S(1)} %shard_map.37) | data formatting | bytes 524288
Async XLA Ops:
  0.0 1.6 %copy-start = (f32[512,128]{1,0:T(8,128)S(1)}, f32[512,128]{1,0:T(8,128)}, u32[]{:S(2)}) copy-start(f32[512,128]{1,0:T(8,128)} %block_ref.1) | copy-start | bytes 786436

commit v8 on v7

--- a/solution.py
+++ b/solution.py
@@ -139,13 +139,25 @@
 
     barrier = pltpu.get_barrier_semaphore()
 
-    @pl.when(r > 0)
-    def _():
-        pl.semaphore_signal(barrier, 1, device_id={"row": r - 1}, device_id_type=MESH)
-
-    @pl.when(r < last)
-    def _():
-        pl.semaphore_signal(barrier, 1, device_id={"row": r + 1}, device_id_type=MESH)
+    def greet(row):
+        pl.semaphore_signal(barrier, 1, device_id={"row": row}, device_id_type=MESH)
+
+    @pl.when(is_first)
+    def _():
+        for row in range(1, n_row):
+            greet(row)
+
+    @pl.when(r > 0)
+    def _():
+        greet(0)
+
+    @pl.when(r > 1)
+    def _():
+        greet(r - 1)
+
+    @pl.when((r > 0) & (r < last))
+    def _():
+        greet(r + 1)
 
     for m in range(1, n_col):
         pl.semaphore_signal(barrier, 1, device_id={"col": (c + m) % n_col}, device_id_type=MESH)
@@ -193,13 +205,8 @@
     def _():
         g[ONE, c] = panels_ref[kc : 2 * kc]
 
-    @pl.when(is_middle)
-    def _():
-        pl.semaphore_wait(barrier, n_col + 1)
-
-    @pl.when(is_first | is_last)
-    def _():
-        pl.semaphore_wait(barrier, n_col)
+    greeted = n_col + jnp.where(r > 1, 1, 0) + jnp.where(r < last, 1, 0)
+    pl.semaphore_wait(barrier, jnp.where(is_first, n_col + n_row - 2, greeted))
 
     def l_copy(d):
         return pltpu.make_async_remote_copy(
@@ -215,10 +222,11 @@
             device_id={"row": r + 1 - 2 * d}, device_id_type=MESH,
         )
 
-    diag_copy = pltpu.make_async_remote_copy(
-        src_ref=d_from, dst_ref=d_from, send_sem=d_sem.at[0], recv_sem=d_sem.at[1],
-        device_id={"row": r + 1}, device_id_type=MESH,
-    )
+    def diag_copy(row):
+        return pltpu.make_async_remote_copy(
+            src_ref=d_from, dst_ref=d_from, send_sem=d_sem.at[0, row], recv_sem=d_sem.at[1, 0],
+            device_id={"row": row}, device_id_type=MESH,
+        )
 
     def arrives(d):
         return jnp.where(d == 0, r > 0, r < last)
@@ -316,7 +324,8 @@
 
     @pl.when(is_first)
     def _():
-        diag_copy.start()
+        for row in range(last, 0, -1):
+            diag_copy(row).start()
         spread_diag()
 
     @pl.when(r > 0)
@@ -353,6 +362,9 @@
 
     @pl.when(r > 0)
     def _():
+        diag_copy(1).wait_recv()
+        spread_diag()
+
         second_c = upright(second)
         q_c = jnp.concatenate([first_c, lookup(second_c == first, lane, second_c, 1)], 0)
         put = one_hot(iota((PW, rows), 1).astype(F32) == second_c - start_f)
@@ -365,16 +377,6 @@
     @pl.when(is_upper)
     def _():
         l_step(1)
-
-    @pl.when(r > 0)
-    def _():
-        diag_copy.wait_recv()
-
-        @pl.when(r < last)
-        def _():
-            diag_copy.start()
-
-        spread_diag()
 
     l_step(0)
 
@@ -513,9 +515,10 @@
     inverse_copy.wait_send()
     drain(TOP)
 
-    @pl.when(r < last)
-    def _():
-        diag_copy.wait_send()
+    @pl.when(is_first)
+    def _():
+        for row in range(1, n_row):
+            diag_copy(row).wait_send()
 
     for d in range(2):
         @pl.when((r < last) if d == 0 else (r > 0))
@@ -533,7 +536,7 @@
     vmem = pl.BlockSpec(memory_space=pltpu.VMEM)
     n_peer = n_col // 2
     dma = pltpu.SemaphoreType.DMA
-    lists = jnp.pad(pivots.astype(F32), ((0, 6), (0, rows - PW)))
+    lists = jnp.pad(pivots, ((0, 6), (0, rows - PW))).astype(F32)
     packed = jnp.concatenate([jnp.swapaxes(panels, 1, 2).reshape(2 * kc, rows), lists], 0)
     return pl.pallas_call(
         functools.partial(kernel, n_row, n_col),
@@ -558,7 +561,7 @@
             pltpu.VMEM((8, rows), F32),
             pltpu.VMEM((tops, rows), BF16),
             pltpu.VMEM((tops, rows), BF16),
-            dma((2,)),
+            dma((2, n_row)),
             dma((2,)),
             dma((2, 2)),
             dma((2, 2, cols // PART)),

time: 26.8 us -> 30 us (1.12)
  Pallas kernels: 24.1 us -> 27 us
    pallas_call x1, Pallas kernels: 24.1 us -> 27 us  [fused(): pl.pallas_call(functools.partial(kernel, n_row, n_col), out_shape=jax.Sha...]
where the time goes in v8:
time: 30 us; the launch traced here: 29.4 us
  Pallas kernels  27 us (90%)
  other arithmetic  1.64 us (5%)
  local copies, waits for them, and re-layouts  0.71 us (2%)
    pallas_call x1, Pallas kernels, fused(): pl.pallas_call(functools.partial(kernel, n_row, n_col), out_shape=jax.Sha...  27 us
    concatenate x1, other arithmetic, fused(): jnp.concatenate([jnp.swapaxes(panels, 1, 2).reshape(2 * kc, rows), lists]...  0.91 us
    convert_element_type x1, other arithmetic, fused(): lists = jnp.pad(pivots, ((0, 6), (0, rows - PW))).astype(F32)  0.73 us
    unnamed x3, local copies, waits for them, and re-layouts  0.71 us

profile of v8, /device:TPU:0, one launch (start us, length us, event | category | flops | bytes accessed | tf_op | source)
XLA Modules:
  0.0 29.4 jit_solution(10079708040260897062)
XLA Ops:
  0.0 0.0 copy-start
  0.0 0.7 %pad_convert_fusion = f32[8,512]{1,0:T(8,128)S(1)} fusion(s32[2,256]{1,0:T(2,128)} %param.5), kind=kLoop, calls=%fused_computation.1 | loop fusion | flops 4096 | bytes 18432 | tf_op jit(solution)/shard_map/convert_element_type | solution.py:539
  0.7 0.9 %pad_maximum_fusion.panels_ref = f32[72,512]{1,0:T(8,128)S(1)} fusion(f32[8,512]{1,0:T(8,128)S(1)} %pad_convert_fusion, f32[64,512]{1,0:T(8,128)} %bitcast.3), kind=kLoop, calls=%fused_computation | loop fusion | flops 36864 | bytes 294912 | tf_op jit(solution)/shard_map/concatenate | solution.py:540
  1.6 0.0 copy-done
  1.7 27.0 %shard_map.37 = f32[512,128]{1,0:T(8,128)S(1)} custom-call(f32[512,128]{1,0:T(8,128)S(1)} %copy-done, f32[72,512]{1,0:T(8,128)S(1)} %pad_maximum_fusion.panels_ref), custom_call_target="tpu_custom_call" | custom-call | tf_op jit(solution)/shard_map/pallas_call | solution.py:541
  28.7 0.7 %copy.5 = f32[512,128]{1,0:T(8,128)} copy(f32[512,128]{1,0:T(8,128)S(1)} %shard_map.37) | data formatting | bytes 524288
Async XLA Ops:
  0.0 1.6 %copy-start = (f32[512,128]{1,0:T(8,128)S(1)}, f32[512,128]{1,0:T(8,128)}, u32[]{:S(2)}) copy-start(f32[512,128]{1,0:T(8,128)} %block_ref.1) | copy-start | bytes 786436

commit v9 on v7

--- a/solution.py
+++ b/solution.py
@@ -351,6 +351,19 @@
         for k in range(chunks):
             f_copy(k, 1).start()
 
+    def pass_diag():
+        diag_copy.wait_recv()
+
+        @pl.when(r < last)
+        def _():
+            diag_copy.start()
+
+        spread_diag()
+
+    @pl.when((r > 0) & jnp.logical_not(is_upper))
+    def _():
+        pass_diag()
+
     @pl.when(r > 0)
     def _():
         second_c = upright(second)
@@ -366,15 +379,9 @@
     def _():
         l_step(1)
 
-    @pl.when(r > 0)
-    def _():
-        diag_copy.wait_recv()
-
-        @pl.when(r < last)
-        def _():
-            diag_copy.start()
-
-        spread_diag()
+    @pl.when(is_upper)
+    def _():
+        pass_diag()
 
     l_step(0)
 
@@ -473,10 +480,7 @@
     inverse_copy.wait_recv()
     inverses = [split(inverse_ref[0]), split(inverse_ref[1])]
 
-    for half in range(2):
-        mine = range(half * chunks // 2, (half + 1) * chunks // 2)
-        at = slice(mine[0] * PART, (mine[-1] + 1) * PART)
-
+    def solve(at, mine):
         @pl.when(is_first)
         def _():
             for k in mine:
@@ -500,6 +504,16 @@
         @pl.when(r > 0)
         def _():
             out_ref[:, at] = (block_t[at] - dot_split(split(upper), (low_high[...], low_low[...]))).T
+
+    @pl.when(is_middle)
+    def _():
+        solve(slice(0, cols), range(0))
+
+    @pl.when(is_first | is_last)
+    def _():
+        for half in range(2):
+            mine = range(half * chunks // 2, (half + 1) * chunks // 2)
+            solve(slice(mine[0] * PART, (mine[-1] + 1) * PART), mine)
 
     @pl.when(r > 0)
     def _():

time: 26.8 us -> 26.6 us (level)
  no operation moved by 1% of the time
where the time goes in v9:
time: 26.6 us; the launch traced here: 26.5 us
  Pallas kernels  24.1 us (91%)
  other arithmetic  1.64 us (6%)
  local copies, waits for them, and re-layouts  0.71 us (3%)
    pallas_call x1, Pallas kernels, fused(): pl.pallas_call(functools.partial(kernel, n_row, n_col), out_shape=jax.Sha...  24.1 us
    concatenate x1, other arithmetic, fused(): jnp.concatenate([jnp.swapaxes(panels, 1, 2).reshape(2 * kc, rows), lists]...  0.91 us
    convert_element_type x1, other arithmetic, fused(): lists = jnp.pad(pivots.astype(F32), ((0, 6), (0, rows - PW)))  0.73 us
    unnamed x3, local copies, waits for them, and re-layouts  0.71 us

profile of v9, /device:TPU:0, one launch (start us, length us, event | category | flops | bytes accessed | tf_op | source)
XLA Modules:
  0.0 26.5 jit_solution(16857934000453034677)
XLA Ops:
  0.0 0.0 copy-start
  0.0 0.7 %convert_element_type.5 = f32[2,256]{1,0:T(2,128)S(1)} convert(s32[2,256]{1,0:T(2,128)} %param.5) | non-fusion elementwise | flops 512 | bytes 4096 | tf_op jit(solution)/shard_map/convert_element_type | solution.py:550
  0.7 0.9 %select_maximum_fusion.panels_ref = f32[72,512]{1,0:T(8,128)S(1)} fusion(f32[2,256]{1,0:T(2,128)S(1)} %convert_element_type.5, f32[64,512]{1,0:T(8,128)} %bitcast.3), kind=kLoop, calls=%fused_computation | loop fusion | flops 110592 | bytes 280576 | tf_op jit(solution)/shard_map/concatenate | solution.py:551
  1.6 0.0 copy-done
  1.7 24.1 %shard_map.37 = f32[512,128]{1,0:T(8,128)S(1)} custom-call(f32[512,128]{1,0:T(8,128)S(1)} %copy-done, f32[72,512]{1,0:T(8,128)S(1)} %select_maximum_fusion.panels_ref), custom_call_target="tpu_custom_call" | custom-call | tf_op jit(solution)/shard_map/pallas_call | solution.py:552
  25.8 0.7 %copy.5 = f32[512,128]{1,0:T(8,128)} copy(f32[512,128]{1,0:T(8,128)S(1)} %shard_map.37) | data formatting | bytes 524288
Async XLA Ops:
  0.0 1.6 %copy-start = (f32[512,128]{1,0:T(8,128)S(1)}, f32[512,128]{1,0:T(8,128)}, u32[]{:S(2)}) copy-start(f32[512,128]{1,0:T(8,128)} %block_ref.1) | copy-start | bytes 786436

commit v10 on v9

--- a/solution.py
+++ b/solution.py
@@ -401,6 +401,7 @@
 
     stage(1)
     stage(2)
+    stage(3)
 
     for m in range(n_peer):
         diag_cross(m).wait_recv()
@@ -417,7 +418,7 @@
         return split(jnp.where(same, jnp.concatenate([small] * (PW // SMALL), 0), 0.0))
 
     power = dot_split(split(small), spaced(small))
-    stage(3)
+    stage(4)
     small = one_hot(lanes % SMALL == iota((SMALL, PW), 0)) - small
     span = 2
     while span < SMALL:
@@ -426,7 +427,7 @@
         small = small + new[:SMALL]
         power = new[SMALL:]
         span *= 2
-        stage(span.bit_length() + 1)
+        stage(span.bit_length() + 2)
     share(TOP)
 
     same = iota((PW, PW), 0) // SMALL == iota((PW, PW), 1) // SMALL
@@ -450,7 +451,7 @@
         right = dot_split(split(beside), split(inverse))
         inverse = inverse - unfold(dot_split(split(fold(inverse)), split(unfold(right))))
         size *= 2
-    for k in range(8, chunks + LAG):
+    for k in range(9, chunks + LAG):
         stage(k)
     inverse_ref[p] = inverse
     inverse_copy.start()

time: 26.6 us -> 26.3 us (0.989)
  Pallas kernels: 24.1 us -> 23.6 us
    pallas_call x1, Pallas kernels: 24.1 us -> 23.6 us  [fused(): pl.pallas_call(functools.partial(kernel, n_row, n_col), out_shape=jax.Sha...]
where the time goes in v10:
time: 26.3 us; the launch traced here: 25.9 us
  Pallas kernels  23.6 us (90%)
  other arithmetic  1.64 us (6%)
  local copies, waits for them, and re-layouts  0.71 us (3%)
    pallas_call x1, Pallas kernels, fused(): pl.pallas_call(functools.partial(kernel, n_row, n_col), out_shape=jax.Sha...  23.6 us
    concatenate x1, other arithmetic, fused(): jnp.concatenate([jnp.swapaxes(panels, 1, 2).reshape(2 * kc, rows), lists]...  0.91 us
    convert_element_type x1, other arithmetic, fused(): lists = jnp.pad(pivots.astype(F32), ((0, 6), (0, rows - PW)))  0.73 us
    unnamed x3, local copies, waits for them, and re-layouts  0.71 us

profile of v10, /device:TPU:0, one launch (start us, length us, event | category | flops | bytes accessed | tf_op | source)
XLA Modules:
  0.0 25.9 jit_solution(11811834725793031071)
XLA Ops:
  0.0 0.0 copy-start
  0.0 0.7 %convert_element_type.5 = f32[2,256]{1,0:T(2,128)S(1)} convert(s32[2,256]{1,0:T(2,128)} %param.5) | non-fusion elementwise | flops 512 | bytes 4096 | tf_op jit(solution)/shard_map/convert_element_type | solution.py:551
  0.7 0.9 %select_maximum_fusion.panels_ref = f32[72,512]{1,0:T(8,128)S(1)} fusion(f32[2,256]{1,0:T(2,128)S(1)} %convert_element_type.5, f32[64,512]{1,0:T(8,128)} %bitcast.3), kind=kLoop, calls=%fused_computation | loop fusion | flops 110592 | bytes 280576 | tf_op jit(solution)/shard_map/concatenate | solution.py:552
  1.6 0.0 copy-done
  1.7 23.6 %shard_map.37 = f32[512,128]{1,0:T(8,128)S(1)} custom-call(f32[512,128]{1,0:T(8,128)S(1)} %copy-done, f32[72,512]{1,0:T(8,128)S(1)} %select_maximum_fusion.panels_ref), custom_call_target="tpu_custom_call" | custom-call | tf_op jit(solution)/shard_map/pallas_call | solution.py:553
  25.2 0.7 %copy.5 = f32[512,128]{1,0:T(8,128)} copy(f32[512,128]{1,0:T(8,128)S(1)} %shard_map.37) | data formatting | bytes 524288
Async XLA Ops:
  0.0 1.6 %copy-start = (f32[512,128]{1,0:T(8,128)S(1)}, f32[512,128]{1,0:T(8,128)}, u32[]{:S(2)}) copy-start(f32[512,128]{1,0:T(8,128)} %block_ref.1) | copy-start | bytes 786436
